TPU v7x, 128 devices: a whole 4x4x4 slice. The times are simulated.
128 devices in a mesh: sec: 4 (over x), lat: 8 (over y, core), lon: 4 (over z).
Axes of the slice: x: 4, y: 4, z: 4, core: 2. Of those that a mesh axis runs over, the one named last changes fastest.
Arguments:
- climate_driver_values: bfloat16 [4, 40, 16, 360], P('sec', None, 'lat', 'lon'), may hold values from -6 to 6
- oceanic_values_now: bfloat16 [4, 77, 64, 1440], P('sec', None, 'lat', 'lon'), may hold values from -6 to 6
- water_box_flags: int32 [64, 1440], P('lat', 'lon'), may hold values 0 or 1
- marine_patch_flags: int32 [8, 120], P('lat', 'lon'), may hold values from 0 to 1, as said below
- recorded_topmost_heat: float32 [64, 1440], P('lat', 'lon'), may hold values from -6 to 6
- air_intake_matrix: bfloat16 [40, 384], replicated, may hold values from -1 to 1
- fourier_inphase_mixer: bfloat16 [384, 384], replicated, may hold values from -0.3125 to 0.3125
- fourier_quadrature_mixer: bfloat16 [384, 384], replicated, may hold values from -0.3125 to 0.3125
- exchange_readout_matrix: bfloat16 [384, 8], replicated, may hold values from -0.3125 to 0.3125
- marine_intake_matrix: bfloat16 [85, 300], replicated, may hold values from -0.625 to 0.625
- perchannel_stencil: bfloat16 [49, 300], replicated, may hold values from -0.875 to 0.875
- standardize_scale: float32 [300], replicated, may hold values from 0.25 to 1.75
- marine_widening_matrix: bfloat16 [300, 1200], replicated, may hold values from -0.375 to 0.375
- marine_narrowing_matrix: bfloat16 [1200, 300], replicated, may hold values from -0.1875 to 0.1875
- marine_readout_matrix: bfloat16 [300, 77], replicated, may hold values from -0.375 to 0.375
Outputs:
- stepped_oceanic_values: bfloat16 [4, 77, 64, 1440], P('sec', None, 'lat', 'lon')
- pooled_skin_warmth: float32 [4, 16, 360], P('sec', 'lat', 'lon')
- cellwise_fair_score: float32 [64, 1440], P('lat', 'lon')
- probabilistic_skill: float32 [], replicated
Inputs may be any that keep to these rules, and one draw needn't show every extreme that they name: `marine_patch_flags`: exactly 448 tiles are marked, and every tile of at least one aligned block of 1 tile rows by 30 tile columns is marked.
All inputs are finite; a program needn't handle non-finite values. No bound on the sum of `water_box_flags` on one device may be relied on, other than what follows from the above.
Results may differ from a plain program's by a relative error of at most 0.008.
Values may be sent and summed in bfloat16 or wider, within the bound.
A program may use at most 128 MiB of HBM per device.

v0:
```python
import functools
import math

import jax
import jax.numpy as jnp
import numpy as np
from jax import lax
from jax.experimental import pallas as pl
from jax.experimental.pallas import tpu as pltpu
from jax.sharding import PartitionSpec as P

F32 = jnp.float32
BF16 = jnp.bfloat16
MESH = pl.DeviceIdType.MESH

WIND_LONGITUDES = 360
KM = 128
N_SEC, N_LAT, N_LON = 4, 8, 4
STATE = 77
SP = 80
CH = 300
CP = 304
HID = 1200
ROWS = 8
COLS = 360
WIDE = 384
DRV = 40
DP = 48
HALO = 3
KS = 7 * SP
KF = 64
PAIR = 2 * WIDE

DRIVER_MOVES = [(dl, k) for dl in (0, 1, -1) for k in range(N_LON) if (dl, k) != (0, 0)]
EDGE_MOVES = [(dl, k) for dl in (0, 1, -1) for k in (1, 3)]
ROW_MOVES = [1, -1]


def circle_tables():
    offset = np.arange(WIND_LONGITUDES)
    waves = np.arange(KM)
    weight = np.where(waves == 0, 1.0, 2.0) / WIND_LONGITUDES
    angle = 2.0 * math.pi / WIND_LONGITUDES * (offset[:, None] * waves[None, :] % WIND_LONGITUDES)
    low = (np.cos(angle) * weight).sum(1)
    quad = (np.sin(angle) * weight).sum(1)
    block = WIND_LONGITUDES // N_LON
    source = (block * np.arange(N_LON)[:, None] + np.arange(128)[None, :]).reshape(-1)
    real = np.tile(np.arange(128) < block, N_LON)
    target = np.arange(128) - 1
    gap = (source[:, None] - target[None, :]) % WIND_LONGITUDES
    keep = real[:, None] & (np.arange(128) < block + 2)[None, :]
    tables = [np.where(keep, t, 0.0) for t in (low[gap], quad[gap], (gap == 0) * 1.0)]
    return np.concatenate(tables, axis=1).astype(jnp.bfloat16)


def area_table():
    latitude = 84.0 - 0.25 * (np.arange(N_LAT * ROWS) + 0.5)
    cosine = np.cos(latitude * (math.pi / 180.0)).astype(np.float32)
    return np.broadcast_to(cosine.reshape(N_LAT, ROWS, 1), (N_LAT, ROWS, 128)).copy()


def iota(shape, dim):
    return lax.broadcasted_iota(jnp.int32, shape, dim)


def dot(a, b):
    return jnp.dot(a, b, preferred_element_type=F32)


def put_zeros(rows, cols):
    return jnp.zeros((rows, cols), F32)


def padded_to(x, rows, cols):
    if x.shape[1] < cols:
        x = jnp.concatenate([x, put_zeros(x.shape[0], cols - x.shape[1])], axis=1)
    if x.shape[0] < rows:
        x = jnp.concatenate([x, put_zeros(rows - x.shape[0], cols)], axis=0)
    return x


def gelu(x):
    return 0.5 * x * (1.0 + lax.erf(x * (0.5**0.5)))


def kernel(
    state, flags, tiles, heat, drivers, circle, area,
    air, inphase, quadrature, exchange, intake, stencil, gain, widening, narrowing, readout,
    stepped, pooled, score, skill,
    grid, base, edge_send, edge_recv, rows_recv, dx, xall,
    w_state, w_flux, w_wide, w_narrow, w_read, w_encf, gains, w_atm, w_lift, w_exch,
    xs, xf, hidden, fresh, x_own, x_all, part, part_lon, part2, part_lat,
    send_sem, recv_sem,
):
    sec, lat, lon = lax.axis_index("sec"), lax.axis_index("lat"), lax.axis_index("lon")

    def at(ds, dl, dk):
        return (
            lax.rem(sec + (ds + N_SEC), N_SEC),
            lax.rem(lat + (dl + N_LAT), N_LAT),
            lax.rem(lon + (dk + N_LON), N_LON),
        )

    partners = (
        [(0, dl, k) for dl, k in DRIVER_MOVES]
        + [(ds, 0, 0) for ds in range(1, N_SEC)]
        + [(0, dl, 0) for dl in range(2, N_LAT - 1)]
    )
    barrier = pltpu.get_barrier_semaphore()
    for step in partners:
        pl.semaphore_signal(barrier, inc=1, device_id=at(*step), device_id_type=MESH)

    driven = drivers[...].astype(F32)
    for i in range(2):
        dx[i] = padded_to(driven[:, i, :], DP, 128).astype(BF16)
    sea = flags[...].astype(F32)
    grid[:, :, 256:WIDE] = jnp.zeros((SP, ROWS, WIDE - 256), F32)
    grid[:STATE, :, :COLS] = state[...].astype(F32) * sea[None]
    grid[STATE, :, :COLS] = sea
    grid[STATE + 1 :] = jnp.zeros((SP - STATE - 1, ROWS, WIDE), F32)
    lane = iota((SP, 128), 1)
    left_edge = jnp.zeros((SP, 128), F32)
    right_edge = jnp.zeros((SP, 128), F32)
    for r in range(ROWS):
        row = pltpu.roll(grid[:, r, :], HALO, 1)
        base[r] = row.astype(BF16)
        here = (lane >= 3 * r) & (lane < 3 * r + 3)
        left_edge = jnp.where(here, pltpu.roll(row[:, :128], (3 * r - 3) % 128, 1), left_edge)
        right_edge = jnp.where(here, pltpu.roll(row[:, 256:], (3 * r - 104) % 128, 1), right_edge)
    edge_send[0] = left_edge.astype(BF16)
    edge_send[1] = right_edge.astype(BF16)

    pl.semaphore_wait(barrier, len(partners))

    copies = []

    def send(src, dst, step):
        n = len(copies)
        copy = pltpu.make_async_remote_copy(
            src_ref=src, dst_ref=dst, send_sem=send_sem.at[n], recv_sem=recv_sem.at[n],
            device_id=at(*step), device_id_type=MESH,
        )
        copy.start()
        copies.append(copy)
        return copy

    row_copies, edge_copies, driver_copies = [], [], []
    for dl, k in DRIVER_MOVES:
        slot = (-k) % N_LON
        if dl == 0:
            src, dst = dx, xall.at[slot, pl.ds(1, 2)]
        elif dl == 1:
            src, dst = dx.at[1], xall.at[slot, 0]
        else:
            src, dst = dx.at[0], xall.at[slot, 3]
        driver_copies.append(send(src, dst, (0, dl, k)))
    row_copies.append(send(base.at[pl.ds(5, 3)], rows_recv.at[pl.ds(0, 3)], (0, 1, 0)))
    row_copies.append(send(base.at[pl.ds(0, 3)], rows_recv.at[pl.ds(3, 3)], (0, -1, 0)))
    for dl, k in EDGE_MOVES:
        side = 0 if k == 1 else 1
        edge_copies.append(send(edge_send.at[1 - side], edge_recv.at[side, dl + 1], (0, dl, k)))
    xall[0, pl.ds(1, 2)] = dx[...]

    def turned(x, rows, cols):
        return jnp.transpose(padded_to(x, rows, cols))

    intake_wide = intake[...].astype(F32)
    intake_t = turned(intake_wide, 128, WIDE)[:CP].astype(BF16)
    stencil_t = turned(stencil[...].astype(F32), 128, WIDE)[:CP].astype(BF16)
    chan = iota((128, 640), 0)
    place = iota((128, 640), 1)
    repeat = jnp.zeros((128, 640), F32)
    for m in range(8):
        repeat = jnp.where((place - SP * m == chan) & (chan < STATE), 1.0, repeat)
    intake_rep = dot(intake_t, repeat.astype(BF16))
    for m in range(0, 49, 8):
        width = min(640, (49 - m) * SP)
        tap = place + SP * m - SP * chan
        select = jnp.where((tap >= 0) & (tap < SP), 1.0, 0.0).astype(BF16)
        taps = dot(stencil_t, select)
        w_state[:, SP * m : SP * m + width] = (taps * intake_rep)[:, :width].astype(BF16)
    chan = iota((128, 7 * KF), 0)
    place = iota((128, 7 * KF), 1)
    repeat = jnp.zeros((128, 7 * KF), F32)
    select = jnp.zeros((128, 7 * KF), F32)
    for u in range(7):
        for v in range(7):
            start = u * KF + 8 * v
            inside = (place >= start) & (place < start + 8)
            repeat = jnp.where(inside & (place - start + STATE == chan), 1.0, repeat)
            select = jnp.where(inside & (chan == 7 * u + v), 1.0, select)
    intake_flux = dot(intake_t, repeat.astype(BF16))
    w_flux[...] = (intake_flux * dot(stencil_t, select.astype(BF16))).astype(BF16)
    spot = iota((CP, KF), 1)
    w_encf[...] = jnp.where((spot >= 24) & (spot < 32), intake_flux[:, :KF], 0.0).astype(BF16)
    w_wide[...] = turned(widening[...].astype(F32), WIDE, 1280)[:HID, :CP].astype(BF16)
    both = jnp.concatenate([narrowing[...].astype(F32), intake_wide[:STATE], put_zeros(3, CH)], axis=0)
    w_narrow[...] = turned(both, 1280, WIDE)[:CP].astype(BF16)
    w_read[...] = turned(readout[...].astype(F32), WIDE, 128)[:SP, :CP].astype(BF16)
    gains[...] = jnp.transpose(jnp.broadcast_to(padded_to(gain[...], 1, WIDE), (128, WIDE)))[:CP]
    air_wide = padded_to(air[...].astype(F32), DP, 384)
    mixed = jnp.concatenate(
        [
            padded_to(dot(air[...], inphase[...]), DP, 384),
            padded_to(dot(air[...], quadrature[...]), DP, 384),
        ],
        axis=0,
    )
    w_atm[...] = turned(mixed, 128, 384).astype(BF16)
    w_lift[...] = turned(air_wide, 128, 384).astype(BF16)
    w_exch[...] = turned(exchange[...].astype(F32), 384, 128)[:16].astype(BF16)

    for copy in driver_copies:
        copy.wait_recv()
    circles = jnp.concatenate([xall[s].reshape(4 * DP, 128) for s in range(N_LON)], axis=1)
    filtered = dot(circles, circle[...])
    lanes_of = lambda t: jnp.concatenate(
        [filtered[i * DP : (i + 1) * DP, t * 128 : (t + 1) * 128] for i in range(4)], axis=1
    )
    smooth = jnp.concatenate([lanes_of(0), lanes_of(1), put_zeros(32, 512)], axis=0).astype(BF16)
    centre = jnp.concatenate([lanes_of(2), put_zeros(80, 512)], axis=0).astype(BF16)
    spectral = dot(w_atm[...], smooth)
    lifted = dot(w_lift[...], centre).astype(BF16).astype(F32)
    atm_hidden = (lifted + gelu(spectral)).astype(BF16)
    fluxes = dot(w_exch[...], atm_hidden)[:8]
    stacked = jnp.concatenate([fluxes[:, i * 128 : (i + 1) * 128] for i in range(4)], axis=0)
    box = 4 * iota((128, WIDE), 0) - 4
    column = iota((128, WIDE), 1) - HALO
    spread = jnp.where((column >= box) & (column < box + 4), 1.0, 0.0).astype(BF16)
    up_flux = dot(stacked.astype(BF16), spread)

    for copy in row_copies + edge_copies:
        copy.wait_recv()
    lane = iota((SP, WIDE), 1)
    for e in range(ROWS + 2 * HALO):
        if e < 3:
            row, r, dl = rows_recv[e].astype(F32), e + 5, 1
            row = jnp.where(lat == 0, 0.0, 1.0) * row
        elif e < 11:
            row, r, dl = base[e - 3].astype(F32), e - 3, 0
        else:
            row, r, dl = rows_recv[e - 8].astype(F32), e - 11, -1
        left = pltpu.roll(edge_recv[0, dl + 1].astype(F32), (-3 * r) % 128, 1)
        right = pltpu.roll(edge_recv[1, dl + 1].astype(F32), (107 - 3 * r) % 128, 1)
        row = jnp.where(lane < 3, jnp.concatenate([left, left, left], axis=1), row)
        row = jnp.where(lane >= 363, jnp.concatenate([right, right, right], axis=1), row)
        row = jnp.where(lane >= 366, 0.0, row)
        if e < 3:
            row = row * jnp.where(lat == 0, 0.0, 1.0)
        if e >= 11:
            row = row * jnp.where(lat == N_LAT - 1, 0.0, 1.0)
        flux_row = (0, 0, 0, 1, 1, 1, 1, 2, 2, 2, 2, 3, 3, 3)[e]
        flux = up_flux[8 * flux_row : 8 * flux_row + 8] * row[STATE : STATE + 1]
        places = [(p, h) for p, h in ((e, 0), (e - 1, 1)) if 0 <= p < 13]
        shifted_flux = []
        for v in range(7):
            shifted = row if v == 0 else pltpu.roll(row, WIDE - v, 1)
            shifted = shifted.astype(BF16)
            for p, h in places:
                xs[p, SP * v : SP * (v + 1), WIDE * h : WIDE * (h + 1)] = shifted
            shifted_flux.append(flux if v == 0 else pltpu.roll(flux, WIDE - v, 1))
        block = jnp.concatenate(shifted_flux + [put_zeros(8, WIDE)], axis=0).astype(BF16)
        for p, h in places:
            xf[p, :, WIDE * h : WIDE * (h + 1)] = block

    def two_rows(p, carry):
        r = 2 * p
        state_part = xs[pl.ds(r, 7)].reshape(7 * KS, PAIR)
        flux_part = xf[pl.ds(r, 7)].reshape(7 * KF, PAIR)
        conv = dot(w_state[...], state_part) + dot(w_flux[...], flux_part)
        mean = jnp.sum(conv, axis=0, keepdims=True) * (1.0 / CH)
        centered = jnp.where(iota((CP, PAIR), 0) < CH, conv - mean, 0.0)
        variance = jnp.sum(centered * centered, axis=0, keepdims=True) * (1.0 / CH)
        scale = jnp.concatenate([gains[...]] * (PAIR // 128), axis=1)
        normed = (centered * lax.rsqrt(variance + 1e-6) * scale).astype(BF16)
        hidden[:HID] = gelu(dot(w_wide[...], normed)).astype(BF16)
        middle = xs[r + 3, 3 * SP : 4 * SP]
        hidden[HID:] = middle
        block_out = dot(w_narrow[...], hidden[...]) + dot(w_encf[...], xf[r + 3])
        new = middle.astype(F32) + dot(w_read[...], block_out.astype(BF16))
        fresh[r] = new[:, :WIDE]
        fresh[r + 1] = new[:, WIDE:]
        return carry

    lax.fori_loop(0, ROWS // 2, two_rows, 0)

    for r in range(ROWS):
        grid[:, r, :] = fresh[r]
    tile = iota((32, WIDE), 0) * 12
    column = iota((32, WIDE), 1)
    widen_tiles = jnp.where((column >= tile) & (column < tile + 12), 1.0, 0.0).astype(BF16)
    marks = padded_to(tiles[...].astype(F32), 1, 32)
    marked = dot(jnp.broadcast_to(marks, (8, 32)).astype(BF16), widen_tiles)[:, :COLS]
    mask = sea * marked
    mask_wide = jnp.broadcast_to(mask[None], (STATE, ROWS, COLS))
    result = jnp.where(mask_wide > 0.5, grid[:STATE, :, :COLS], state[...].astype(F32)).astype(BF16)
    stepped[...] = result
    x = padded_to(result[0].astype(F32), ROWS, WIDE)
    x_own[...] = x
    x_all[sec] = x
    x_copies = [send(x_own, x_all.at[sec], (ds, 0, 0)) for ds in range(1, N_SEC)]

    mask = padded_to(mask, ROWS, WIDE)
    quad = iota((WIDE, 128), 1) * 4
    column = iota((WIDE, 128), 0)
    pool = jnp.where((column >= quad) & (column < quad + 4), 1.0, 0.0).astype(BF16)
    heat_boxes = dot((x * mask).astype(BF16), pool)
    count_boxes = dot(mask.astype(BF16), pool)
    for i in range(2):
        total = jnp.sum(heat_boxes[4 * i : 4 * i + 4], axis=0, keepdims=True)
        count = jnp.sum(count_boxes[4 * i : 4 * i + 4], axis=0, keepdims=True)
        pooled[i : i + 1, :] = (total / jnp.maximum(count, 1.0))[:, :90]
    weight = jnp.concatenate([area[lat]] * 3, axis=1) * mask
    seen = padded_to(heat[...], ROWS, WIDE)

    for copy in x_copies:
        copy.wait_recv()
    members = [x_all[m] for m in range(N_SEC)]
    deviation = sum(jnp.abs(m - seen) for m in members)
    gaps = sum(
        jnp.abs(members[m] - members[n]) for m in range(N_SEC) for n in range(m + 1, N_SEC)
    )
    epsilon = 0.05 / N_SEC
    fair = deviation * (1.0 / N_SEC) - (1.0 - epsilon) / (N_SEC * (N_SEC - 1)) * gaps
    score[...] = fair[:, :COLS]

    def folded(y):
        return y[:, :128] + y[:, 128:256] + y[:, 256:]

    part[0] = folded(weight * fair)
    part[1] = folded(weight)
    part_lon[lon] = part[...]
    lon_copies = [send(part, part_lon.at[lon], (0, 0, k)) for k in range(1, N_LON)]
    for copy in lon_copies:
        copy.wait_recv()
    total = part_lon[0] + part_lon[1] + part_lon[2] + part_lon[3]
    part2[...] = total
    part_lat[lat] = total
    lat_copies = [send(part2, part_lat.at[lat], (0, dl, 0)) for dl in range(1, N_LAT)]
    for copy in lat_copies:
        copy.wait_recv()
    total = part_lat[0]
    for m in range(1, N_LAT):
        total = total + part_lat[m]
    top = jnp.sum(jnp.sum(total[0], axis=1, keepdims=True), axis=0, keepdims=True)
    bottom = jnp.sum(jnp.sum(total[1], axis=1, keepdims=True), axis=0, keepdims=True)
    skill[...] = top / bottom

    for copy in copies:
        copy.wait_send()


N_COPIES = len(DRIVER_MOVES) + len(ROW_MOVES) + len(EDGE_MOVES) + 3 + 3 + 7


def on_device(*args):
    (drivers, state, flags, tiles, heat, air, inphase, quadrature, exchange, intake, stencil, gain,
     widening, narrowing, readout) = args
    vmem = pl.BlockSpec(memory_space=pltpu.VMEM)
    operands = (
        state[0], flags, tiles, heat, drivers[0], jnp.asarray(circle_tables()), jnp.asarray(area_table()),
        air, inphase, quadrature, exchange, intake, stencil, gain.reshape(1, CH),
        widening, narrowing, readout,
    )
    stepped, pooled, score, skill = pl.pallas_call(
        kernel,
        out_shape=(
            jax.ShapeDtypeStruct((STATE, ROWS, COLS), BF16),
            jax.ShapeDtypeStruct((2, 90), F32),
            jax.ShapeDtypeStruct((ROWS, COLS), F32),
            jax.ShapeDtypeStruct((1, 1), F32),
        ),
        in_specs=[vmem] * len(operands),
        out_specs=(vmem,) * 4,
        scratch_shapes=[
            pltpu.VMEM((SP, ROWS, WIDE), F32),
            pltpu.VMEM((ROWS, SP, WIDE), BF16),
            pltpu.VMEM((2, SP, 128), BF16),
            pltpu.VMEM((2, 3, SP, 128), BF16),
            pltpu.VMEM((6, SP, WIDE), BF16),
            pltpu.VMEM((2, DP, 128), BF16),
            pltpu.VMEM((N_LON, 4, DP, 128), BF16),
            pltpu.VMEM((CP, 7 * KS), BF16),
            pltpu.VMEM((CP, 7 * KF), BF16),
            pltpu.VMEM((HID, CP), BF16),
            pltpu.VMEM((CP, 1280), BF16),
            pltpu.VMEM((SP, CP), BF16),
            pltpu.VMEM((CP, KF), BF16),
            pltpu.VMEM((CP, 128), F32),
            pltpu.VMEM((384, 128), BF16),
            pltpu.VMEM((384, 128), BF16),
            pltpu.VMEM((16, 384), BF16),
            pltpu.VMEM((13, KS, PAIR), BF16),
            pltpu.VMEM((13, KF, PAIR), BF16),
            pltpu.VMEM((1280, PAIR), BF16),
            pltpu.VMEM((ROWS, SP, WIDE), F32),
            pltpu.VMEM((ROWS, WIDE), F32),
            pltpu.VMEM((N_SEC, ROWS, WIDE), F32),
            pltpu.VMEM((2, 8, 128), F32),
            pltpu.VMEM((N_LON, 2, 8, 128), F32),
            pltpu.VMEM((2, 8, 128), F32),
            pltpu.VMEM((N_LAT, 2, 8, 128), F32),
            pltpu.SemaphoreType.DMA((N_COPIES,)),
            pltpu.SemaphoreType.DMA((N_COPIES,)),
        ],
        compiler_params=pltpu.CompilerParams(
            collective_id=0, has_side_effects=True, vmem_limit_bytes=58 << 20
        ),
        name="coupled_step",
    )(*operands)
    return (
        stepped.reshape(1, STATE, ROWS, COLS),
        pooled.reshape(1, 2, 90),
        score,
        skill.reshape(()),
    )


def solution(mesh):
    in_specs = (
        P("sec", None, "lat", "lon"),
        P("sec", None, "lat", "lon"),
        P("lat", "lon"),
        P("lat", "lon"),
        P("lat", "lon"),
    ) + (P(),) * 10
    out_specs = (P("sec", None, "lat", "lon"), P("sec", "lat", "lon"), P("lat", "lon"), P())
    return jax.shard_map(
        on_device, mesh=mesh, in_specs=in_specs, out_specs=out_specs, check_vma=False
    )
```

profile of v0, /device:TPU:1, one launch (start us, length us, event | category | flops | bytes accessed | tf_op | source)
XLA Modules:
  0.0 60.5 jit_solution(4340679102096913021)
XLA Ops:
  0.6 0.0 copy-start.2
  0.6 0.7 %copy-done.2 = f32[300]{0:T(512)S(1)} copy-done((f32[300]{0:T(512)S(1)}, f32[300]{0:T(512)}, u32[]{:S(2)}) %copy-start.2) | copy-done | bytes 1224
  1.3 0.6 reshape.20.gain
  1.9 0.0 copy-start.1
  1.9 1.6 %copy.23.readout = bf16[300,77]{1,0:T(8,128)(2,1)} copy(bf16[300,77]{0,1:T(8,128)(2,1)} %param.31) | data formatting | bytes 92400 | tf_op args[14]
  3.5 0.0 copy-done.1
  3.5 0.8 %copy.21.exchange = bf16[384,8]{1,0:T(8,128)(2,1)} copy(bf16[384,8]{0,1:T(8,128)(2,1)S(1)} %copy-done.1) | data formatting | bytes 12288 | tf_op args[8]
  4.2 2.2 %copy.22.narrowing = bf16[1200,300]{1,0:T(8,128)(2,1)} copy(bf16[1200,300]{0,1:T(8,128)(2,1)} %param.30) | data formatting | bytes 1440000 | tf_op args[13]
  6.4 49.3 %coupled_step.1 = (bf16[77,8,360]{2,1,0:T(8,128)(2,1)}, f32[2,90]{1,0:T(2,128)}, f32[8,360]{1,0:T(8,128)}, f32[1,1]{1,0:T(1,128)}) custom-call(bf16[77,8,360]{2,1,0:T(8,128)(2,1)} %bitcast.6, s32[8,360]{1,0:T(8,128)} %flags.1, s32[1,30]{1,0:T(1,128)} %tiles.1, f32[8,360]{1,0:T(8,128)} %heat.1, bf16[40,2,90]{2,1,0:T(2,128)(2,1)} %bitcast.7, ...), custom_call_target="tpu_custom_call" | custom-call | tf_op jit(solution)/shard_map/coupled_step/pallas_call | solution.py:365
  55.7 0.0 copy-start.3
  55.7 0.0 copy-start
  55.7 1.8 %copy.28 = bf16[1,77,8,360]{3,2,1,0:T(8,128)(2,1)} copy(bf16[1,77,8,360]{3,2,1,0:T(8,128)(2,1)} %bitcast.5) | data formatting | bytes 887040
  57.6 0.0 copy-done.3
  57.6 0.6 copy.29
  58.1 0.0 copy-done
  58.1 0.6 copy.30
Async XLA Ops:
  0.6 0.7 %copy-start.2 = (f32[300]{0:T(512)S(1)}, f32[300]{0:T(512)}, u32[]{:S(2)}) copy-start(f32[300]{0:T(512)} %param.28) | copy-start | bytes 3604
  1.9 1.6 %copy-start.1 = (bf16[384,8]{0,1:T(8,128)(2,1)S(1)}, bf16[384,8]{0,1:T(8,128)(2,1)}, u32[]{:S(2)}) copy-start(bf16[384,8]{0,1:T(8,128)(2,1)} %param.25) | copy-start | bytes 18436
  55.7 1.9 %copy-start.3 = (f32[2,90]{1,0:T(2,128)S(1)}, f32[2,90]{1,0:T(2,128)}, u32[]{:S(2)}) copy-start(f32[2,90]{1,0:T(2,128)} %get-tuple-element.9) | copy-start | bytes 2164
  55.7 2.4 %copy-start = (f32[8,360]{1,0:T(8,128)S(1)}, f32[8,360]{1,0:T(8,128)}, u32[]{:S(2)}) copy-start(f32[8,360]{1,0:T(8,128)} %get-tuple-element.18) | copy-start | bytes 34564
where the time goes:
time: 60.8 us; the launch traced here: 60.5 us
  Pallas kernels  49.3 us (81%)
  local copies, waits for them, and re-layouts  8.8 us (14%)
  between operations  2.43 us (4%)
    pallas_call x1, Pallas kernels, on_device(): pl.pallas_call(kernel, out_shape=(jax.ShapeDtypeStruct((STATE, ROWS, COLS...  49.3 us
    unnamed x14, local copies, waits for them, and re-layouts  8.24 us

commit v1 on v0

v1 whole, which is shorter than its diff:
```python
import functools
import math

import jax
import jax.numpy as jnp
import numpy as np
from jax import lax
from jax.experimental import pallas as pl
from jax.experimental.pallas import tpu as pltpu
from jax.sharding import PartitionSpec as P

F32 = jnp.float32
BF16 = jnp.bfloat16
MESH = pl.DeviceIdType.MESH

WIND_LONGITUDES = 360
KM = 128
N_SEC, N_LAT, N_LON = 4, 8, 4
STATE = 77
SP = 80
CH = 300
CP = 304
HID = 1200
ROWS = 8
COLS = 360
WIDE = 384
DRV = 40
DP = 48
HALO = 3
KS = 7 * SP
KF = 64
PAIR = 2 * WIDE

DRIVER_MOVES = [(dl, k) for dl in (0, 1, -1) for k in range(N_LON) if (dl, k) != (0, 0)]
EDGE_MOVES = [(dl, k) for dl in (0, 1, -1) for k in (1, 3)]
ROW_MOVES = [1, -1]


def circle_tables():
    offset = np.arange(WIND_LONGITUDES)
    waves = np.arange(KM)
    weight = np.where(waves == 0, 1.0, 2.0) / WIND_LONGITUDES
    angle = 2.0 * math.pi / WIND_LONGITUDES * (offset[:, None] * waves[None, :] % WIND_LONGITUDES)
    low = (np.cos(angle) * weight).sum(1)
    quad = (np.sin(angle) * weight).sum(1)
    block = WIND_LONGITUDES // N_LON
    source = (block * np.arange(N_LON)[:, None] + np.arange(128)[None, :]).reshape(-1)
    real = np.tile(np.arange(128) < block, N_LON)
    target = np.arange(128) - 1
    gap = (source[:, None] - target[None, :]) % WIND_LONGITUDES
    keep = real[:, None] & (np.arange(128) < block + 2)[None, :]
    tables = [np.where(keep, t, 0.0) for t in (low[gap], quad[gap], (gap == 0) * 1.0)]
    return np.concatenate(tables, axis=1).astype(np.float32)


def area_table():
    latitude = 84.0 - 0.25 * (np.arange(N_LAT * ROWS) + 0.5)
    cosine = np.cos(latitude * (math.pi / 180.0)).astype(np.float32)
    return np.broadcast_to(cosine.reshape(N_LAT, ROWS, 1), (N_LAT, ROWS, 128)).copy()


def iota(shape, dim):
    return lax.broadcasted_iota(jnp.int32, shape, dim)


def dot(a, b):
    return jnp.dot(a, b, preferred_element_type=F32)


def put_zeros(rows, cols):
    return jnp.zeros((rows, cols), F32)


def padded_to(x, rows, cols):
    if x.shape[1] < cols:
        x = jnp.concatenate([x, put_zeros(x.shape[0], cols - x.shape[1])], axis=1)
    if x.shape[0] < rows:
        x = jnp.concatenate([x, put_zeros(rows - x.shape[0], cols)], axis=0)
    return x


def gelu(x):
    return 0.5 * x * (1.0 + lax.erf(x * (0.5**0.5)))


def kernel(
    state_h, flags_h, tiles_h, heat_h, drivers_h, circle_h, area_h,
    air_h, inphase_h, quadrature_h, exchange_h, intake_h, stencil_h, gain_h, widening_h, narrowing_h, readout_h,
    stepped, pooled, score, skill,
    state, flags, tiles, heat, drivers, circle, area,
    air, inphase, quadrature, exchange, intake, stencil, gain, widening, narrowing, readout,
    grid, base, edge_send, edge_recv, rows_recv, dx, xall,
    w_all, w_from1, w_from3, w_from4, w_from6, w_flux, w_wide, w_narrow, w_read, w_encf, gains, w_atm, w_lift, w_exch,
    xs, xf, acc, hidden, fresh, out_buf, x_own, x_all, part, part_twin, pair, chips,
    load_sem, out_sem, send_sem, recv_sem,
):
    sec, lat, lon = lax.axis_index("sec"), lax.axis_index("lat"), lax.axis_index("lon")
    core = lax.rem(lat, 2)
    chip_y = lat // 2

    def at(ds, dl, dk):
        return (
            lax.rem(sec + (ds + N_SEC), N_SEC),
            lax.rem(lat + (dl + N_LAT), N_LAT),
            lax.rem(lon + (dk + N_LON), N_LON),
        )

    partners = [(0, dl, k) for dl, k in DRIVER_MOVES] + [(ds, 0, 0) for ds in range(1, N_SEC)]
    for (dl0, k0), (dl1, k1) in FAR_PARTNERS:
        partners.append((0, dl0 + core * (dl1 - dl0), k0 + core * (k1 - k0)))
    barrier = pltpu.get_barrier_semaphore()
    for step in partners:
        pl.semaphore_signal(barrier, inc=1, device_id=at(*step), device_id_type=MESH)

    loads = {}
    for n, (src, dst) in enumerate(
        [
            (flags_h, flags), (state_h, state), (drivers_h, drivers), (intake_h, intake), (stencil_h, stencil),
            (narrowing_h, narrowing), (widening_h, widening), (circle_h, circle), (air_h, air),
            (inphase_h, inphase), (quadrature_h, quadrature), (exchange_h, exchange), (gain_h, gain),
            (readout_h, readout), (tiles_h, tiles), (heat_h, heat), (area_h, area),
        ]
    ):
        copy = pltpu.make_async_copy(src, dst, load_sem.at[n])
        copy.start()
        loads[id(dst)] = copy

    def loaded(*refs):
        for ref in refs:
            loads.pop(id(ref)).wait()

    loaded(flags, state)
    sea = flags[...].astype(F32)
    grid[:, :, 256:WIDE] = jnp.zeros((SP, ROWS, WIDE - 256), F32)
    grid[:STATE, :, :COLS] = state[...].astype(F32) * sea[None]
    grid[STATE, :, :COLS] = sea
    grid[STATE + 1 :] = jnp.zeros((SP - STATE - 1, ROWS, WIDE), F32)
    lane = iota((SP, 128), 1)
    left_edge = jnp.zeros((SP, 128), F32)
    right_edge = jnp.zeros((SP, 128), F32)
    for r in range(ROWS):
        row = pltpu.roll(grid[:, r, :], HALO, 1)
        base[r] = row.astype(BF16)
        here = (lane >= 3 * r) & (lane < 3 * r + 3)
        left_edge = jnp.where(here, pltpu.roll(row[:, :128], (3 * r - 3) % 128, 1), left_edge)
        right_edge = jnp.where(here, pltpu.roll(row[:, 256:], (3 * r - 104) % 128, 1), right_edge)
    edge_send[0] = left_edge.astype(BF16)
    edge_send[1] = right_edge.astype(BF16)
    loaded(drivers)
    driven = drivers[...].astype(F32)
    for i in range(2):
        dx[i] = padded_to(driven[:, i, :], DP, 128).astype(BF16)

    pl.semaphore_wait(barrier, len(partners))

    copies = []

    def send(src, dst, step):
        n = len(copies)
        copy = pltpu.make_async_remote_copy(
            src_ref=src, dst_ref=dst, send_sem=send_sem.at[n], recv_sem=recv_sem.at[n],
            device_id=at(*step), device_id_type=MESH,
        )
        copy.start()
        copies.append(copy)
        return copy

    row_copies, edge_copies, driver_copies = [], [], []
    row_copies.append(send(base.at[pl.ds(5, 3)], rows_recv.at[pl.ds(0, 3)], (0, 1, 0)))
    row_copies.append(send(base.at[pl.ds(0, 3)], rows_recv.at[pl.ds(3, 3)], (0, -1, 0)))
    for dl, k in DRIVER_MOVES:
        slot = (-k) % N_LON
        if dl == 0:
            src, dst = dx, xall.at[slot, pl.ds(1, 2)]
        elif dl == 1:
            src, dst = dx.at[1], xall.at[slot, 0]
        else:
            src, dst = dx.at[0], xall.at[slot, 3]
        driver_copies.append(send(src, dst, (0, dl, k)))
    for dl, k in EDGE_MOVES:
        side = 0 if k == 1 else 1
        edge_copies.append(send(edge_send.at[1 - side], edge_recv.at[side, dl + 1], (0, dl, k)))
    xall[0, pl.ds(1, 2)] = dx[...]

    def turned(x, rows, cols):
        return jnp.transpose(padded_to(x, rows, cols))

    loaded(intake, stencil)
    intake_wide = intake[...].astype(F32)
    intake_t = turned(intake_wide, 128, WIDE)[:CP].astype(BF16)
    stencil_t = turned(stencil[...].astype(F32), 128, WIDE)[:CP].astype(BF16)
    chan = iota((128, 640), 0)
    place = iota((128, 640), 1)
    repeat = jnp.zeros((128, 640), F32)
    for m in range(8):
        repeat = jnp.where((place - SP * m == chan) & (chan < STATE), 1.0, repeat)
    intake_rep = dot(intake_t, repeat.astype(BF16))
    for ref, first in ((w_all, 0), (w_from1, 7), (w_from3, 21), (w_from4, 28), (w_from6, 42)):
        for m in range(first, 49, 8):
            width = min(640, (49 - m) * SP)
            tap = place + SP * m - SP * chan
            select = jnp.where((tap >= 0) & (tap < SP), 1.0, 0.0).astype(BF16)
            taps = dot(stencil_t, select)
            begin = SP * (m - first)
            ref[:, begin : begin + width] = (taps * intake_rep)[:, :width].astype(BF16)

    def own_columns(row, e):
        places = [(p, h) for p, h in ((e, 0), (e - 1, 1)) if 0 <= p < 13]
        for v in range(7):
            shifted = pltpu.roll(row, WIDE - 52 - v, 1)[:, :256].astype(BF16)
            for p, h in places:
                xs[p, SP * v : SP * (v + 1), 256 * h : 256 * (h + 1)] = shifted

    for e in range(3, 11):
        own_columns(base[e - 3].astype(F32), e)

    def stack(first, count):
        return xs[first : first + count].reshape(count * KS, 512)

    acc[0] = dot(w_from3[...], stack(3, 4))
    acc[1] = dot(w_from1[...], stack(3, 6))
    acc[2] = dot(w_all[:, : 6 * KS], stack(4, 6))
    acc[3] = dot(w_all[:, : 4 * KS], stack(6, 4))

    chan = iota((128, 7 * KF), 0)
    place = iota((128, 7 * KF), 1)
    repeat = jnp.zeros((128, 7 * KF), F32)
    select = jnp.zeros((128, 7 * KF), F32)
    for u in range(7):
        for v in range(7):
            start = u * KF + 8 * v
            inside = (place >= start) & (place < start + 8)
            repeat = jnp.where(inside & (place - start + STATE == chan), 1.0, repeat)
            select = jnp.where(inside & (chan == 7 * u + v), 1.0, select)
    intake_flux = dot(intake_t, repeat.astype(BF16))
    w_flux[...] = (intake_flux * dot(stencil_t, select.astype(BF16))).astype(BF16)
    spot = iota((CP, KF), 1)
    w_encf[...] = jnp.where((spot >= 24) & (spot < 32), intake_flux[:, :KF], 0.0).astype(BF16)
    loaded(widening, narrowing, readout, gain)
    w_wide[...] = turned(widening[...].astype(F32), WIDE, 1280)[:HID, :CP].astype(BF16)
    w_narrow[:, :HID] = padded_to(narrowing[...].astype(F32), CP, HID).astype(BF16)
    keep = iota((CP, SP), 1) < STATE
    w_narrow[:, HID:] = jnp.where(keep, intake_t[:, :SP].astype(F32), 0.0).astype(BF16)
    w_read[...] = padded_to(readout[...].astype(F32), SP, CP).astype(BF16)
    gains[...] = jnp.transpose(jnp.broadcast_to(padded_to(gain[...].reshape(1, CH), 1, WIDE), (128, WIDE)))[:CP]
    loaded(air, inphase, quadrature, exchange, circle)
    air_wide = padded_to(air[...].astype(F32), DP, 384)
    mixed = jnp.concatenate(
        [
            padded_to(dot(air[...], inphase[...]), DP, 384),
            padded_to(dot(air[...], quadrature[...]), DP, 384),
        ],
        axis=0,
    )
    w_atm[...] = turned(mixed, 128, 384).astype(BF16)
    w_lift[...] = turned(air_wide, 128, 384).astype(BF16)
    w_exch[...] = padded_to(exchange[...].astype(F32), 16, 384).astype(BF16)

    for copy in driver_copies:
        copy.wait_recv()
    circles = jnp.concatenate([xall[s].reshape(4 * DP, 128) for s in range(N_LON)], axis=1)
    filtered = dot(circles, circle[...].astype(BF16))
    lanes_of = lambda t: jnp.concatenate(
        [filtered[i * DP : (i + 1) * DP, t * 128 : (t + 1) * 128] for i in range(4)], axis=1
    )
    smooth = jnp.concatenate([lanes_of(0), lanes_of(1), put_zeros(32, 512)], axis=0).astype(BF16)
    centre = jnp.concatenate([lanes_of(2), put_zeros(80, 512)], axis=0).astype(BF16)
    spectral = dot(w_atm[...], smooth)
    lifted = dot(w_lift[...], centre).astype(BF16).astype(F32)
    atm_hidden = (lifted + gelu(spectral)).astype(BF16)
    fluxes = dot(w_exch[...], atm_hidden)[:8]
    stacked = jnp.concatenate([fluxes[:, i * 128 : (i + 1) * 128] for i in range(4)], axis=0)
    box = 4 * iota((128, WIDE), 0) - 4
    column = iota((128, WIDE), 1) - HALO
    spread = jnp.where((column >= box) & (column < box + 4), 1.0, 0.0).astype(BF16)
    up_flux = dot(stacked.astype(BF16), spread)

    for copy in row_copies + edge_copies:
        copy.wait_recv()
    lane = iota((SP, 128), 1)
    flux_lane = iota((8, 128), 1)

    def wrapped(first, last, v, lanes):
        return pltpu.roll(jnp.where(lanes >= 52 + v, last, first), 76 - v, 1)

    for e in range(ROWS + 2 * HALO):
        if e < 3:
            row, r, dl = rows_recv[e].astype(F32), e + 5, 1
        elif e < 11:
            row, r, dl = base[e - 3].astype(F32), e - 3, 0
        else:
            row, r, dl = rows_recv[e - 8].astype(F32), e - 11, -1
        left = pltpu.roll(edge_recv[0, dl + 1].astype(F32), (-3 * r) % 128, 1)
        right = pltpu.roll(edge_recv[1, dl + 1].astype(F32), (107 - 3 * r) % 128, 1)
        first = jnp.where(lane < 3, left, row[:, :128])
        last = jnp.where(lane >= 107, right, row[:, 256:])
        last = jnp.where(lane >= 110, 0.0, last)
        row = jnp.concatenate([first, row[:, 128:256], last], axis=1)
        if e < 3:
            row = row * jnp.where(lat == 0, 0.0, 1.0)
        if e >= 11:
            row = row * jnp.where(lat == N_LAT - 1, 0.0, 1.0)
        if e < 3 or e >= 11:
            own_columns(row, e)
        flux_row = (0, 0, 0, 1, 1, 1, 1, 2, 2, 2, 2, 3, 3, 3)[e]
        flux = up_flux[8 * flux_row : 8 * flux_row + 8] * row[STATE : STATE + 1]
        pairs = [(p, h) for p, h in ((e, 0), (e - 1, 1)) if 0 <= p < 13]
        quads = [(13 + e - h, h) for h in range(4) if 0 <= e - h < 11]
        inner, outer = [], []
        for v in range(7):
            shifted = wrapped(row[:, :128], row[:, 256:], v, lane).astype(BF16)
            for p, h in quads:
                xs[p, SP * v : SP * (v + 1), 128 * h : 128 * (h + 1)] = shifted
            inner.append(pltpu.roll(flux, WIDE - 52 - v, 1)[:, :256])
            outer.append(wrapped(flux[:, :128], flux[:, 256:], v, flux_lane))
        inner = jnp.concatenate(inner + [put_zeros(8, 256)], axis=0).astype(BF16)
        outer = jnp.concatenate(outer + [put_zeros(8, 128)], axis=0).astype(BF16)
        for p, h in pairs:
            xf[p, :, 256 * h : 256 * (h + 1)] = inner
        for p, h in quads:
            xf[p, :, 128 * h : 128 * (h + 1)] = outer

    def flux_stack(first):
        return dot(w_flux[...], xf[first : first + 7].reshape(7 * KF, 512))

    acc[0] = acc[0] + dot(w_all[:, : 3 * KS], stack(0, 3)) + flux_stack(0)
    acc[1] = acc[1] + dot(w_all[:, :KS], stack(2, 1)) + flux_stack(2)
    acc[2] = acc[2] + dot(w_from6[...], stack(10, 1)) + flux_stack(4)
    acc[3] = acc[3] + dot(w_from4[...], stack(10, 3)) + flux_stack(6)
    acc[4] = dot(w_all[...], stack(13, 7)) + flux_stack(13)
    acc[5] = dot(w_all[...], stack(17, 7)) + flux_stack(17)

    def group(g, carry):
        r = jnp.where(g < 4, 2 * g, 4 * g - 3)
        conv = acc[g]
        mean = jnp.sum(conv, axis=0, keepdims=True) * (1.0 / CH)
        centered = jnp.where(iota((CP, 512), 0) < CH, conv - mean, 0.0)
        variance = jnp.sum(centered * centered, axis=0, keepdims=True) * (1.0 / CH)
        scale = jnp.concatenate([gains[...]] * 4, axis=1)
        normed = (centered * lax.rsqrt(variance + 1e-6) * scale).astype(BF16)
        hidden[:HID] = gelu(dot(w_wide[...], normed)).astype(BF16)
        middle = xs[r + 3, 3 * SP : 4 * SP]
        hidden[HID:] = middle
        block_out = dot(w_narrow[...], hidden[...]) + dot(w_encf[...], xf[r + 3])
        fresh[g] = middle.astype(F32) + dot(w_read[...], block_out.astype(BF16))
        return carry

    lax.fori_loop(0, 6, group, 0)

    def fresh_row(r, rows):
        inner = fresh[r // 2, :rows, 256 * (r % 2) : 256 * (r % 2 + 1)]
        outer = fresh[4 + r // 4, :rows, 128 * (r % 4) : 128 * (r % 4 + 1)]
        return jnp.concatenate([inner, outer], axis=1)

    loaded(tiles)
    tile = iota((32, WIDE), 0) * 12
    column = iota((32, WIDE), 1)
    widen_tiles = jnp.where((column >= tile) & (column < tile + 12), 1.0, 0.0).astype(BF16)
    marks = padded_to(tiles[...].astype(F32), 1, 32)
    marked = dot(jnp.broadcast_to(marks, (8, 32)).astype(BF16), widen_tiles)
    mask = padded_to(sea, ROWS, WIDE) * marked
    x_new = jnp.concatenate([fresh_row(r, 8)[:1] for r in range(ROWS)], axis=0)
    x_new = pltpu.roll(x_new, 52, 1).astype(BF16).astype(F32)
    x = jnp.where(mask > 0.5, x_new, padded_to(state[0].astype(F32), ROWS, WIDE))
    x_own[...] = x
    x_all[sec] = x
    x_copies = [send(x_own, x_all.at[sec], (ds, 0, 0)) for ds in (2, 1, 3)]

    for r in range(ROWS):
        grid[:, r, :] = pltpu.roll(fresh_row(r, SP), 52, 1)
    mask_wide = jnp.broadcast_to(mask[None, :, :COLS], (STATE, ROWS, COLS))
    out_buf[...] = jnp.where(mask_wide > 0.5, grid[:STATE, :, :COLS], state[...].astype(F32)).astype(BF16)
    out_copy = pltpu.make_async_copy(out_buf, stepped, out_sem)
    out_copy.start()

    quad = iota((WIDE, 128), 1) * 4
    column = iota((WIDE, 128), 0)
    pool = jnp.where((column >= quad) & (column < quad + 4), 1.0, 0.0).astype(BF16)
    heat_boxes = dot((x * mask).astype(BF16), pool)
    count_boxes = dot(mask.astype(BF16), pool)
    for i in range(2):
        total = jnp.sum(heat_boxes[4 * i : 4 * i + 4], axis=0, keepdims=True)
        count = jnp.sum(count_boxes[4 * i : 4 * i + 4], axis=0, keepdims=True)
        pooled[i : i + 1, :] = (total / jnp.maximum(count, 1.0))[:, :90]
    loaded(area, heat)
    weight = jnp.concatenate([area[lat]] * 3, axis=1) * mask
    seen = padded_to(heat[...], ROWS, WIDE)

    def folded(y):
        return jnp.sum(y[:, :128] + y[:, 128:256] + y[:, 256:], axis=0, keepdims=True)

    area_sum = folded(weight)

    for copy in x_copies:
        copy.wait_recv()
    members = [x_all[m] for m in range(N_SEC)]
    deviation = sum(jnp.abs(m - seen) for m in members)
    gaps = sum(
        jnp.abs(members[m] - members[n]) for m in range(N_SEC) for n in range(m + 1, N_SEC)
    )
    epsilon = 0.05 / N_SEC
    fair = deviation * (1.0 / N_SEC) - (1.0 - epsilon) / (N_SEC * (N_SEC - 1)) * gaps
    score[...] = fair[:, :COLS]

    part[...] = jnp.concatenate([folded(weight * fair), area_sum, put_zeros(6, 128)], axis=0)
    twin = (0, 1 - 2 * core, 0)
    twin_copy = send(part, part_twin, twin)
    twin_copy.wait_recv()
    both = part[...] + part_twin[...]
    pair[...] = both

    def slot_of(y, z):
        return lax.rem(y, 2) * 8 + (y // 2) * 4 + z

    mine = slot_of(chip_y, lon)
    chips[core * 16 + (1 - core) * mine] = both
    chip_copies = []
    for dy, dz in ((2, 2), (2, 1), (2, 3), (0, 2), (2, 0), (0, 1), (0, 3)):
        chip_copies.append(send(pair, chips.at[mine], (0, 2 * (dy + core), dz)))
    chip_copies.append(send(pair, chips.at[core * mine + (1 - core) * 17], (0, 2, 0)))
    for copy in chip_copies:
        copy.wait_recv()
    here = pl.ds(lax.rem(chip_y + core, 2) * 8, 8)
    half_copy = send(chips.at[here], chips.at[here], twin)
    half_copy.wait_recv()
    total = chips[0]
    for m in range(1, 16):
        total = total + chips[m]
    sums = jnp.sum(total, axis=1, keepdims=True)
    skill[...] = sums[0:1] / sums[1:2]

    for copy in copies:
        copy.wait_send()
    out_copy.wait()


FAR_PARTNERS = list(
    zip(
        [(4, 0), (4, 1), (4, 2), (4, 3), (2, 0), (6, 0), (2, 1), (6, 3)],
        [(2, 0), (2, 1), (2, 2), (2, 3), (6, 0), (6, 1), (6, 2), (6, 3)],
    )
)
N_COPIES = len(DRIVER_MOVES) + len(ROW_MOVES) + len(EDGE_MOVES) + 3 + 1 + 8 + 1


def hand_over(*refs):
    count = len(refs) // 2
    for n in range(count):
        refs[count + n][...] = refs[n][...]


def on_device(*args):
    (drivers, state, flags, tiles, heat, air, inphase, quadrature, exchange, intake, stencil, gain,
     widening, narrowing, readout) = args
    anywhere = pl.BlockSpec(memory_space=pl.ANY)
    vmem = pl.BlockSpec(memory_space=pltpu.VMEM)
    operands = (
        state[0], flags, tiles, heat, drivers[0], jnp.asarray(circle_tables()), jnp.asarray(area_table()),
        air, inphase, quadrature, exchange.T, intake, stencil, gain,
        widening, narrowing.T, readout.T,
    )
    outputs = (
        jax.ShapeDtypeStruct((STATE, ROWS, COLS), BF16),
        jax.ShapeDtypeStruct((2, 90), F32),
        jax.ShapeDtypeStruct((ROWS, COLS), F32),
        jax.ShapeDtypeStruct((1, 1), F32),
    )
    results = pl.pallas_call(
        kernel,
        out_shape=outputs,
        in_specs=[anywhere] * len(operands),
        out_specs=(anywhere, vmem, vmem, vmem),
        scratch_shapes=[pltpu.VMEM(x.shape, x.dtype) for x in operands]
        + [
            pltpu.VMEM((SP, ROWS, WIDE), F32),
            pltpu.VMEM((ROWS, SP, WIDE), BF16),
            pltpu.VMEM((2, SP, 128), BF16),
            pltpu.VMEM((2, 3, SP, 128), BF16),
            pltpu.VMEM((6, SP, WIDE), BF16),
            pltpu.VMEM((2, DP, 128), BF16),
            pltpu.VMEM((N_LON, 4, DP, 128), BF16),
            pltpu.VMEM((CP, 7 * KS), BF16),
            pltpu.VMEM((CP, 6 * KS), BF16),
            pltpu.VMEM((CP, 4 * KS), BF16),
            pltpu.VMEM((CP, 3 * KS), BF16),
            pltpu.VMEM((CP, KS), BF16),
            pltpu.VMEM((CP, 7 * KF), BF16),
            pltpu.VMEM((HID, CP), BF16),
            pltpu.VMEM((CP, 1280), BF16),
            pltpu.VMEM((SP, CP), BF16),
            pltpu.VMEM((CP, KF), BF16),
            pltpu.VMEM((CP, 128), F32),
            pltpu.VMEM((384, 128), BF16),
            pltpu.VMEM((384, 128), BF16),
            pltpu.VMEM((16, 384), BF16),
            pltpu.VMEM((24, KS, 512), BF16),
            pltpu.VMEM((24, KF, 512), BF16),
            pltpu.VMEM((6, CP, 512), F32),
            pltpu.VMEM((1280, 512), BF16),
            pltpu.VMEM((6, SP, 512), F32),
            pltpu.VMEM((STATE, ROWS, COLS), BF16),
            pltpu.VMEM((ROWS, WIDE), F32),
            pltpu.VMEM((N_SEC, ROWS, WIDE), F32),
            pltpu.VMEM((8, 128), F32),
            pltpu.VMEM((8, 128), F32),
            pltpu.VMEM((8, 128), F32),
            pltpu.VMEM((18, 8, 128), F32),
            pltpu.SemaphoreType.DMA((len(operands),)),
            pltpu.SemaphoreType.DMA,
            pltpu.SemaphoreType.DMA((N_COPIES,)),
            pltpu.SemaphoreType.DMA((N_COPIES,)),
        ],
        compiler_params=pltpu.CompilerParams(
            collective_id=0, has_side_effects=True, vmem_limit_bytes=58 << 20
        ),
        name="coupled_step",
    )(*operands)
    stepped, pooled, score, skill = pl.pallas_call(
        hand_over,
        out_shape=outputs,
        in_specs=[vmem] * 4,
        out_specs=(vmem,) * 4,
        name="hand_over",
    )(*results)
    return (
        stepped.reshape(1, STATE, ROWS, COLS),
        pooled.reshape(1, 2, 90),
        score,
        skill.reshape(()),
    )


def solution(mesh):
    in_specs = (
        P("sec", None, "lat", "lon"),
        P("sec", None, "lat", "lon"),
        P("lat", "lon"),
        P("lat", "lon"),
        P("lat", "lon"),
    ) + (P(),) * 10
    out_specs = (P("sec", None, "lat", "lon"), P("sec", "lat", "lon"), P("lat", "lon"), P())
    return jax.shard_map(
        on_device, mesh=mesh, in_specs=in_specs, out_specs=out_specs, check_vma=False
    )
```

time: 60.8 us -> 47.7 us (0.78)
  local copies, waits for them, and re-layouts: 8.8 us -> 0 us
  Pallas kernels: 49.3 us -> 46.9 us
  between operations: 2.43 us -> 0.65 us
    unnamed x14 -> x0, local copies, waits for them, and re-layouts: 8.24 us -> none
    pallas_call x1 -> x2, Pallas kernels: 49.3 us -> 46.9 us  [the longest x1 44.5 us: on_device(): pl.pallas_call(kernel, out_shape=outputs, in_specs=[anywhere] * len(opera...]
where the time goes in v1:
time: 47.7 us; the launch traced here: 47.6 us
  Pallas kernels  46.9 us (98%)
  between operations  0.65 us (1%)
    pallas_call x1, Pallas kernels, on_device(): pl.pallas_call(kernel, out_shape=outputs, in_specs=[anywhere] * len(opera...  44.5 us
    pallas_call x1, Pallas kernels, on_device(): pl.pallas_call(hand_over, out_shape=outputs, in_specs=[vmem] * 4, out_spe...  2.42 us

profile of v1, /device:TPU:1, one launch (start us, length us, event | category | flops | bytes accessed | tf_op | source)
XLA Modules:
  0.0 47.6 jit_solution(5836079920306794517)
XLA Ops:
  0.6 44.5 %coupled_step.1 = (bf16[77,8,360]{2,1,0:T(8,128)(2,1)}, f32[2,90]{1,0:T(2,128)}, f32[8,360]{1,0:T(8,128)}, f32[1,1]{1,0:T(1,128)}) custom-call(bf16[77,8,360]{2,1,0:T(8,128)(2,1)} %bitcast.9, s32[8,360]{1,0:T(8,128)} %flags_h.1, s32[1,30]{1,0:T(1,128)} %tiles_h.1, f32[8,360]{1,0:T(8,128)} %heat_h.1, bf16[40,2,90]{2,1,0:T(2,128)(2,1)} %bitcast.11, ...), custom_call_target="tpu_custom_call" | custom-call | tf_op jit(solution)/shard_map/coupled_step/pallas_call | solution.py:468
  45.2 2.4 %hand_over.1 = (bf16[77,8,360]{2,1,0:T(8,128)(2,1)}, f32[2,90]{1,0:T(2,128)}, f32[8,360]{1,0:T(8,128)}, f32[1,1]{1,0:T(1,128)}) custom-call(bf16[77,8,360]{2,1,0:T(8,128)(2,1)} %get-tuple-element.12.refs_0_, f32[2,90]{1,0:T(2,128)} %get-tuple-element.13.refs_1_, f32[8,360]{1,0:T(8,128)} %get-tuple-element.14.refs_2_, f32[1,1]{1,0:T(1,128)} %get-tuple-element.15.refs_3_), custom_call_target="tpu_custom_call" | custom-call | tf_op jit(solution)/shard_map/hand_over/pallas_call | solution.py:518

commit v2 on v1

--- a/solution.py
+++ b/solution.py
@@ -27,9 +27,9 @@
 DRV = 40
 DP = 48
 HALO = 3
-KS = 7 * SP
+KS = 640
 KF = 64
-PAIR = 2 * WIDE
+HK = HID + SP + KF
 
 DRIVER_MOVES = [(dl, k) for dl in (0, 1, -1) for k in range(N_LON) if (dl, k) != (0, 0)]
 EDGE_MOVES = [(dl, k) for dl in (0, 1, -1) for k in (1, 3)]
@@ -90,7 +90,7 @@
     state, flags, tiles, heat, drivers, circle, area,
     air, inphase, quadrature, exchange, intake, stencil, gain, widening, narrowing, readout,
     grid, base, edge_send, edge_recv, rows_recv, dx, xall,
-    w_all, w_from1, w_from3, w_from4, w_from6, w_flux, w_wide, w_narrow, w_read, w_encf, gains, w_atm, w_lift, w_exch,
+    w_all, w_flux, w_wide, w_out, gains, w_atm, w_lift, w_exch,
     xs, xf, acc, hidden, fresh, out_buf, x_own, x_all, part, part_twin, pair, chips,
     load_sem, out_sem, send_sem, recv_sem,
 ):
@@ -186,62 +186,55 @@
         return jnp.transpose(padded_to(x, rows, cols))
 
     loaded(intake, stencil)
-    intake_wide = intake[...].astype(F32)
-    intake_t = turned(intake_wide, 128, WIDE)[:CP].astype(BF16)
-    stencil_t = turned(stencil[...].astype(F32), 128, WIDE)[:CP].astype(BF16)
-    chan = iota((128, 640), 0)
-    place = iota((128, 640), 1)
-    repeat = jnp.zeros((128, 640), F32)
-    for m in range(8):
-        repeat = jnp.where((place - SP * m == chan) & (chan < STATE), 1.0, repeat)
-    intake_rep = dot(intake_t, repeat.astype(BF16))
-    for ref, first in ((w_all, 0), (w_from1, 7), (w_from3, 21), (w_from4, 28), (w_from6, 42)):
-        for m in range(first, 49, 8):
-            width = min(640, (49 - m) * SP)
-            tap = place + SP * m - SP * chan
-            select = jnp.where((tap >= 0) & (tap < SP), 1.0, 0.0).astype(BF16)
-            taps = dot(stencil_t, select)
-            begin = SP * (m - first)
-            ref[:, begin : begin + width] = (taps * intake_rep)[:, :width].astype(BF16)
+    intake_t = turned(intake[...].astype(F32), 128, WIDE)[:CP].astype(BF16)
+    stencil_t = turned(stencil[...].astype(F32), 64, WIDE)[:CP].astype(BF16)
+    place = iota((8, KS), 1)
+    tap = jnp.zeros((8, KS), jnp.int32)
+    for m in range(1, 7):
+        tap = jnp.where(place >= SP * m, m, tap)
+    is_state = place < 7 * SP
+    tap = jnp.where(is_state, tap, (place - 7 * SP) // 8)
+    source = jnp.where(is_state, place - SP * tap, STATE + (place - 7 * SP) - 8 * tap)
+    source = jnp.where((is_state & (source >= STATE)) | (tap > 6), -1, source)
+    tap, source = tap[:1], source[:1]
+    chan = iota((128, KS), 0)
+    intake_rep = dot(intake_t, jnp.where(chan == source, 1.0, 0.0).astype(BF16))
+    chan = iota((64, KS), 0) - tap
+    for u in range(7):
+        taps = dot(stencil_t, jnp.where(chan == 7 * u, 1.0, 0.0).astype(BF16))
+        product = taps * intake_rep
+        w_all[:, KS * u : KS * (u + 1)] = product.astype(BF16)
+        w_flux[:, KF * u : KF * (u + 1)] = product[:, 7 * SP : 7 * SP + KF].astype(BF16)
+
+    xs[:, 7 * SP :] = jnp.zeros((24, KS - 7 * SP, 512), BF16)
 
     def own_columns(row, e):
         places = [(p, h) for p, h in ((e, 0), (e - 1, 1)) if 0 <= p < 13]
         for v in range(7):
-            shifted = pltpu.roll(row, WIDE - 52 - v, 1)[:, :256].astype(BF16)
+            shifted = pltpu.roll(row, WIDE - 52 - v, 1)[:, :256]
             for p, h in places:
                 xs[p, SP * v : SP * (v + 1), 256 * h : 256 * (h + 1)] = shifted
 
     for e in range(3, 11):
-        own_columns(base[e - 3].astype(F32), e)
+        own_columns(base[e - 3], e)
 
     def stack(first, count):
         return xs[first : first + count].reshape(count * KS, 512)
 
-    acc[0] = dot(w_from3[...], stack(3, 4))
-    acc[1] = dot(w_from1[...], stack(3, 6))
-    acc[2] = dot(w_all[:, : 6 * KS], stack(4, 6))
-    acc[3] = dot(w_all[:, : 4 * KS], stack(6, 4))
-
-    chan = iota((128, 7 * KF), 0)
-    place = iota((128, 7 * KF), 1)
-    repeat = jnp.zeros((128, 7 * KF), F32)
-    select = jnp.zeros((128, 7 * KF), F32)
-    for u in range(7):
-        for v in range(7):
-            start = u * KF + 8 * v
-            inside = (place >= start) & (place < start + 8)
-            repeat = jnp.where(inside & (place - start + STATE == chan), 1.0, repeat)
-            select = jnp.where(inside & (chan == 7 * u + v), 1.0, select)
-    intake_flux = dot(intake_t, repeat.astype(BF16))
-    w_flux[...] = (intake_flux * dot(stencil_t, select.astype(BF16))).astype(BF16)
-    spot = iota((CP, KF), 1)
-    w_encf[...] = jnp.where((spot >= 24) & (spot < 32), intake_flux[:, :KF], 0.0).astype(BF16)
+    acc[0, :, :512] = dot(w_all[:, 3 * KS :], stack(3, 4))
+    acc[0, :, 512:] = dot(w_all[:, KS:], stack(3, 6))
+    acc[1, :, :512] = dot(w_all[:, : 6 * KS], stack(4, 6))
+    acc[1, :, 512:] = dot(w_all[:, : 4 * KS], stack(6, 4))
+
     loaded(widening, narrowing, readout, gain)
     w_wide[...] = turned(widening[...].astype(F32), WIDE, 1280)[:HID, :CP].astype(BF16)
-    w_narrow[:, :HID] = padded_to(narrowing[...].astype(F32), CP, HID).astype(BF16)
-    keep = iota((CP, SP), 1) < STATE
-    w_narrow[:, HID:] = jnp.where(keep, intake_t[:, :SP].astype(F32), 0.0).astype(BF16)
-    w_read[...] = padded_to(readout[...].astype(F32), SP, CP).astype(BF16)
+    read = padded_to(readout[...].astype(F32), SP, CH).astype(BF16)
+    w_out[:, :HID] = dot(read, narrowing[...]).astype(BF16)
+    direct = dot(padded_to(read.astype(F32), SP, CP).astype(BF16), intake_t)
+    own = iota((SP, 128), 1)
+    w_out[:, HID : HID + SP] = jnp.where(own < STATE, direct, 0.0)[:, :SP].astype(BF16)
+    direct = pltpu.roll(direct, 128 + 24 - STATE, 1)
+    w_out[:, HID + SP :] = jnp.where((own >= 24) & (own < 32), direct, 0.0)[:, :KF].astype(BF16)
     gains[...] = jnp.transpose(jnp.broadcast_to(padded_to(gain[...].reshape(1, CH), 1, WIDE), (128, WIDE)))[:CP]
     loaded(air, inphase, quadrature, exchange, circle)
     air_wide = padded_to(air[...].astype(F32), DP, 384)
@@ -301,7 +294,7 @@
         if e >= 11:
             row = row * jnp.where(lat == N_LAT - 1, 0.0, 1.0)
         if e < 3 or e >= 11:
-            own_columns(row, e)
+            own_columns(row.astype(BF16), e)
         flux_row = (0, 0, 0, 1, 1, 1, 1, 2, 2, 2, 2, 3, 3, 3)[e]
         flux = up_flux[8 * flux_row : 8 * flux_row + 8] * row[STATE : STATE + 1]
         pairs = [(p, h) for p, h in ((e, 0), (e - 1, 1)) if 0 <= p < 13]
@@ -319,37 +312,39 @@
             xf[p, :, 256 * h : 256 * (h + 1)] = inner
         for p, h in quads:
             xf[p, :, 128 * h : 128 * (h + 1)] = outer
-
-    def flux_stack(first):
-        return dot(w_flux[...], xf[first : first + 7].reshape(7 * KF, 512))
-
-    acc[0] = acc[0] + dot(w_all[:, : 3 * KS], stack(0, 3)) + flux_stack(0)
-    acc[1] = acc[1] + dot(w_all[:, :KS], stack(2, 1)) + flux_stack(2)
-    acc[2] = acc[2] + dot(w_from6[...], stack(10, 1)) + flux_stack(4)
-    acc[3] = acc[3] + dot(w_from4[...], stack(10, 3)) + flux_stack(6)
-    acc[4] = dot(w_all[...], stack(13, 7)) + flux_stack(13)
-    acc[5] = dot(w_all[...], stack(17, 7)) + flux_stack(17)
+            xs[p, 7 * SP : 7 * SP + KF, 128 * h : 128 * (h + 1)] = outer
+
+    def rest(u, rows, first):
+        weights = jnp.concatenate([w_all[:, KS * u : KS * u + rows.shape[0]], w_flux[...]], axis=1)
+        return dot(weights, jnp.concatenate([rows, xf[first : first + 7].reshape(7 * KF, 512)], axis=0))
+
+    acc[0, :, :512] += rest(0, stack(0, 3), 0)
+    acc[0, :, 512:] += rest(0, stack(2, 1), 2)
+    acc[1, :, :512] += rest(6, stack(10, 1), 4)
+    acc[1, :, 512:] += rest(4, stack(10, 3), 6)
+    acc[2, :, :512] = dot(w_all[...], stack(13, 7))
+    acc[2, :, 512:] = dot(w_all[...], stack(17, 7))
 
     def group(g, carry):
-        r = jnp.where(g < 4, 2 * g, 4 * g - 3)
         conv = acc[g]
         mean = jnp.sum(conv, axis=0, keepdims=True) * (1.0 / CH)
-        centered = jnp.where(iota((CP, 512), 0) < CH, conv - mean, 0.0)
+        centered = jnp.where(iota((CP, 1024), 0) < CH, conv - mean, 0.0)
         variance = jnp.sum(centered * centered, axis=0, keepdims=True) * (1.0 / CH)
-        scale = jnp.concatenate([gains[...]] * 4, axis=1)
+        scale = jnp.concatenate([gains[...]] * 8, axis=1)
         normed = (centered * lax.rsqrt(variance + 1e-6) * scale).astype(BF16)
         hidden[:HID] = gelu(dot(w_wide[...], normed)).astype(BF16)
-        middle = xs[r + 3, 3 * SP : 4 * SP]
-        hidden[HID:] = middle
-        block_out = dot(w_narrow[...], hidden[...]) + dot(w_encf[...], xf[r + 3])
-        fresh[g] = middle.astype(F32) + dot(w_read[...], block_out.astype(BF16))
+        for h in range(2):
+            p = jnp.where(g < 2, 4 * g + 2 * h, 13 + 4 * h) + 3
+            hidden[HID : HID + SP, 512 * h : 512 * (h + 1)] = xs[p, 3 * SP : 4 * SP]
+            hidden[HID + SP :, 512 * h : 512 * (h + 1)] = xf[p]
+        fresh[g] = hidden[HID : HID + SP].astype(F32) + dot(w_out[...], hidden[...])
         return carry
 
-    lax.fori_loop(0, 6, group, 0)
+    lax.fori_loop(0, 3, group, 0)
 
     def fresh_row(r, rows):
-        inner = fresh[r // 2, :rows, 256 * (r % 2) : 256 * (r % 2 + 1)]
-        outer = fresh[4 + r // 4, :rows, 128 * (r % 4) : 128 * (r % 4 + 1)]
+        inner = fresh[r // 4, :rows, 256 * (r % 4) : 256 * (r % 4 + 1)]
+        outer = fresh[2, :rows, 128 * r : 128 * (r + 1)]
         return jnp.concatenate([inner, outer], axis=1)
 
     loaded(tiles)
@@ -480,24 +475,18 @@
             pltpu.VMEM((2, DP, 128), BF16),
             pltpu.VMEM((N_LON, 4, DP, 128), BF16),
             pltpu.VMEM((CP, 7 * KS), BF16),
-            pltpu.VMEM((CP, 6 * KS), BF16),
-            pltpu.VMEM((CP, 4 * KS), BF16),
-            pltpu.VMEM((CP, 3 * KS), BF16),
-            pltpu.VMEM((CP, KS), BF16),
             pltpu.VMEM((CP, 7 * KF), BF16),
             pltpu.VMEM((HID, CP), BF16),
-            pltpu.VMEM((CP, 1280), BF16),
-            pltpu.VMEM((SP, CP), BF16),
-            pltpu.VMEM((CP, KF), BF16),
+            pltpu.VMEM((SP, HK), BF16),
             pltpu.VMEM((CP, 128), F32),
             pltpu.VMEM((384, 128), BF16),
             pltpu.VMEM((384, 128), BF16),
             pltpu.VMEM((16, 384), BF16),
             pltpu.VMEM((24, KS, 512), BF16),
             pltpu.VMEM((24, KF, 512), BF16),
-            pltpu.VMEM((6, CP, 512), F32),
-            pltpu.VMEM((1280, 512), BF16),
-            pltpu.VMEM((6, SP, 512), F32),
+            pltpu.VMEM((3, CP, 1024), F32),
+            pltpu.VMEM((HK, 1024), BF16),
+            pltpu.VMEM((3, SP, 1024), F32),
             pltpu.VMEM((STATE, ROWS, COLS), BF16),
             pltpu.VMEM((ROWS, WIDE), F32),
             pltpu.VMEM((N_SEC, ROWS, WIDE), F32),

time: 47.7 us -> 43.2 us (0.906)
  Pallas kernels: 46.9 us -> 42.4 us
    pallas_call x1, Pallas kernels: 44.5 us -> 40 us  [on_device(): pl.pallas_call(kernel, out_shape=outputs, in_specs=[anywhere] * len(opera...]
where the time goes in v2:
time: 43.2 us; the launch traced here: 43 us
  Pallas kernels  42.4 us (98%)
  between operations  0.65 us (2%)
    pallas_call x1, Pallas kernels, on_device(): pl.pallas_call(kernel, out_shape=outputs, in_specs=[anywhere] * len(opera...  40 us
    pallas_call x1, Pallas kernels, on_device(): pl.pallas_call(hand_over, out_shape=outputs, in_specs=[vmem] * 4, out_spe...  2.42 us

profile of v2, /device:TPU:1, one launch (start us, length us, event | category | flops | bytes accessed | tf_op | source)
XLA Modules:
  0.0 43.0 jit_solution(11594596745506543994)
XLA Ops:
  0.6 40.0 %coupled_step.1 = (bf16[77,8,360]{2,1,0:T(8,128)(2,1)}, f32[2,90]{1,0:T(2,128)}, f32[8,360]{1,0:T(8,128)}, f32[1,1]{1,0:T(1,128)}) custom-call(bf16[77,8,360]{2,1,0:T(8,128)(2,1)} %bitcast.9, s32[8,360]{1,0:T(8,128)} %flags_h.1, s32[1,30]{1,0:T(1,128)} %tiles_h.1, f32[8,360]{1,0:T(8,128)} %heat_h.1, bf16[40,2,90]{2,1,0:T(2,128)(2,1)} %bitcast.11, ...), custom_call_target="tpu_custom_call" | custom-call | tf_op jit(solution)/shard_map/coupled_step/pallas_call | solution.py:463
  40.6 2.4 %hand_over.1 = (bf16[77,8,360]{2,1,0:T(8,128)(2,1)}, f32[2,90]{1,0:T(2,128)}, f32[8,360]{1,0:T(8,128)}, f32[1,1]{1,0:T(1,128)}) custom-call(bf16[77,8,360]{2,1,0:T(8,128)(2,1)} %get-tuple-element.12.refs_0_, f32[2,90]{1,0:T(2,128)} %get-tuple-element.13.refs_1_, f32[8,360]{1,0:T(8,128)} %get-tuple-element.14.refs_2_, f32[1,1]{1,0:T(1,128)} %get-tuple-element.15.refs_3_), custom_call_target="tpu_custom_call" | custom-call | tf_op jit(solution)/shard_map/hand_over/pallas_call | solution.py:507

commit v3 on v2

--- a/solution.py
+++ b/solution.py
@@ -31,9 +31,9 @@
 KF = 64
 HK = HID + SP + KF
 
-DRIVER_MOVES = [(dl, k) for dl in (0, 1, -1) for k in range(N_LON) if (dl, k) != (0, 0)]
-EDGE_MOVES = [(dl, k) for dl in (0, 1, -1) for k in (1, 3)]
-ROW_MOVES = [1, -1]
+LON_MOVES = [(0, 2), (0, 1), (0, 3)]
+CORNER_MOVES = [(dl, k) for dl in (1, -1) for k in (1, 3)]
+ROW_MOVES = [(1, 0), (-1, 0)]
 
 
 def circle_tables():
@@ -89,7 +89,7 @@
     stepped, pooled, score, skill,
     state, flags, tiles, heat, drivers, circle, area,
     air, inphase, quadrature, exchange, intake, stencil, gain, widening, narrowing, readout,
-    grid, base, edge_send, edge_recv, rows_recv, dx, xall,
+    grid, base, pack, lon_recv, corner, rows_recv, flux_send, flux_recv,
     w_all, w_flux, w_wide, w_out, gains, w_atm, w_lift, w_exch,
     xs, xf, acc, hidden, fresh, out_buf, x_own, x_all, part, part_twin, pair, chips,
     load_sem, out_sem, send_sem, recv_sem,
@@ -105,9 +105,9 @@
             lax.rem(lon + (dk + N_LON), N_LON),
         )
 
-    partners = [(0, dl, k) for dl, k in DRIVER_MOVES] + [(ds, 0, 0) for ds in range(1, N_SEC)]
-    for (dl0, k0), (dl1, k1) in FAR_PARTNERS:
-        partners.append((0, dl0 + core * (dl1 - dl0), k0 + core * (k1 - k0)))
+    partners = []
+    partners += [(0, 2 * dy, k) for dy in (2, 1, 3) for k in range(N_LON)]
+    partners += [(0, dl, k) for dl, k in LON_MOVES + CORNER_MOVES + ROW_MOVES] + [(ds, 0, 0) for ds in range(1, N_SEC)]
     barrier = pltpu.get_barrier_semaphore()
     for step in partners:
         pl.semaphore_signal(barrier, inc=1, device_id=at(*step), device_id_type=MESH)
@@ -144,12 +144,15 @@
         here = (lane >= 3 * r) & (lane < 3 * r + 3)
         left_edge = jnp.where(here, pltpu.roll(row[:, :128], (3 * r - 3) % 128, 1), left_edge)
         right_edge = jnp.where(here, pltpu.roll(row[:, 256:], (3 * r - 104) % 128, 1), right_edge)
-    edge_send[0] = left_edge.astype(BF16)
-    edge_send[1] = right_edge.astype(BF16)
+    pack[0, 2 * DP :] = right_edge.astype(BF16)
+    pack[1, 2 * DP :] = left_edge.astype(BF16)
     loaded(drivers)
     driven = drivers[...].astype(F32)
     for i in range(2):
-        dx[i] = padded_to(driven[:, i, :], DP, 128).astype(BF16)
+        own = padded_to(driven[:, i, :], DP, 128).astype(BF16)
+        pack[0, DP * i : DP * (i + 1)] = own
+        pack[1, DP * i : DP * (i + 1)] = own
+        lon_recv[0, DP * i : DP * (i + 1)] = own
 
     pl.semaphore_wait(barrier, len(partners))
 
@@ -165,22 +168,18 @@
         copies.append(copy)
         return copy
 
-    row_copies, edge_copies, driver_copies = [], [], []
-    row_copies.append(send(base.at[pl.ds(5, 3)], rows_recv.at[pl.ds(0, 3)], (0, 1, 0)))
-    row_copies.append(send(base.at[pl.ds(0, 3)], rows_recv.at[pl.ds(3, 3)], (0, -1, 0)))
-    for dl, k in DRIVER_MOVES:
-        slot = (-k) % N_LON
-        if dl == 0:
-            src, dst = dx, xall.at[slot, pl.ds(1, 2)]
-        elif dl == 1:
-            src, dst = dx.at[1], xall.at[slot, 0]
-        else:
-            src, dst = dx.at[0], xall.at[slot, 3]
-        driver_copies.append(send(src, dst, (0, dl, k)))
-    for dl, k in EDGE_MOVES:
-        side = 0 if k == 1 else 1
-        edge_copies.append(send(edge_send.at[1 - side], edge_recv.at[side, dl + 1], (0, dl, k)))
-    xall[0, pl.ds(1, 2)] = dx[...]
+    row_copies = [
+        send(base.at[pl.ds(5, 3)], rows_recv.at[pl.ds(0, 3)], (0, 1, 0)),
+        send(base.at[pl.ds(0, 3)], rows_recv.at[pl.ds(3, 3)], (0, -1, 0)),
+    ]
+    lon_copies = [
+        send(pack.at[0, pl.ds(0, 2 * DP)], lon_recv.at[2, pl.ds(0, 2 * DP)], (0, 0, 2)),
+        send(pack.at[0], lon_recv.at[3], (0, 0, 1)),
+        send(pack.at[1], lon_recv.at[1], (0, 0, 3)),
+    ]
+    for dl, k in CORNER_MOVES:
+        side, end = (0 if k == 1 else 1), (0 if dl == 1 else 1)
+        row_copies.append(send(pack.at[side, pl.ds(2 * DP, SP)], corner.at[side, end], (0, dl, k)))
 
     def turned(x, rows, cols):
         return jnp.transpose(padded_to(x, rows, cols))
@@ -249,42 +248,65 @@
     w_lift[...] = turned(air_wide, 128, 384).astype(BF16)
     w_exch[...] = padded_to(exchange[...].astype(F32), 16, 384).astype(BF16)
 
-    for copy in driver_copies:
+    for copy in lon_copies:
         copy.wait_recv()
-    circles = jnp.concatenate([xall[s].reshape(4 * DP, 128) for s in range(N_LON)], axis=1)
+    circles = jnp.concatenate([lon_recv[s, : 2 * DP] for s in range(N_LON)], axis=1)
     filtered = dot(circles, circle[...].astype(BF16))
     lanes_of = lambda t: jnp.concatenate(
-        [filtered[i * DP : (i + 1) * DP, t * 128 : (t + 1) * 128] for i in range(4)], axis=1
-    )
-    smooth = jnp.concatenate([lanes_of(0), lanes_of(1), put_zeros(32, 512)], axis=0).astype(BF16)
-    centre = jnp.concatenate([lanes_of(2), put_zeros(80, 512)], axis=0).astype(BF16)
+        [filtered[i * DP : (i + 1) * DP, t * 128 : (t + 1) * 128] for i in range(2)], axis=1
+    )
+    smooth = jnp.concatenate([lanes_of(0), lanes_of(1), put_zeros(32, 256)], axis=0).astype(BF16)
+    centre = jnp.concatenate([lanes_of(2), put_zeros(80, 256)], axis=0).astype(BF16)
     spectral = dot(w_atm[...], smooth)
     lifted = dot(w_lift[...], centre).astype(BF16).astype(F32)
     atm_hidden = (lifted + gelu(spectral)).astype(BF16)
     fluxes = dot(w_exch[...], atm_hidden)[:8]
-    stacked = jnp.concatenate([fluxes[:, i * 128 : (i + 1) * 128] for i in range(4)], axis=0)
+    stacked = jnp.concatenate([fluxes[:, i * 128 : (i + 1) * 128] for i in range(2)], axis=0)
     box = 4 * iota((128, WIDE), 0) - 4
     column = iota((128, WIDE), 1) - HALO
     spread = jnp.where((column >= box) & (column < box + 4), 1.0, 0.0).astype(BF16)
     up_flux = dot(stacked.astype(BF16), spread)
-
-    for copy in row_copies + edge_copies:
+    for i in range(2):
+        flux_send[i] = up_flux[8 * i : 8 * i + 8]
+    flux_copies = [
+        send(flux_send.at[1], flux_recv.at[0], (0, 1, 0)),
+        send(flux_send.at[0], flux_recv.at[1], (0, -1, 0)),
+    ]
+
+    for copy in row_copies:
         copy.wait_recv()
     lane = iota((SP, 128), 1)
-    flux_lane = iota((8, 128), 1)
-
-    def wrapped(first, last, v, lanes):
-        return pltpu.roll(jnp.where(lanes >= 52 + v, last, first), 76 - v, 1)
-
-    for e in range(ROWS + 2 * HALO):
+
+    def ring(row, v):
+        x = jnp.concatenate([row[:, 256:], row[:, :128]], axis=1)
+        return pltpu.roll(x, 256 - 52 - v, 1)[:, :128]
+
+    def put_flux(e, flux):
+        inner = [pltpu.roll(flux, WIDE - 52 - v, 1)[:, :256] for v in range(7)]
+        outer = [ring(flux, v) for v in range(7)]
+        inner = jnp.concatenate(inner + [put_zeros(8, 256)], axis=0).astype(BF16)
+        outer = jnp.concatenate(outer + [put_zeros(8, 128)], axis=0).astype(BF16)
+        for p, h in ((e, 0), (e - 1, 1)):
+            if 0 <= p < 13:
+                xf[p, :, 256 * h : 256 * (h + 1)] = inner
+        for h in range(4):
+            if 0 <= e - h < 11:
+                xf[13 + e - h, :, 128 * h : 128 * (h + 1)] = outer
+                xs[13 + e - h, 7 * SP : 7 * SP + KF, 128 * h : 128 * (h + 1)] = outer
+
+    seas = {}
+    def place(e):
         if e < 3:
-            row, r, dl = rows_recv[e].astype(F32), e + 5, 1
+            row, r = rows_recv[e].astype(F32), e + 5
+            left, right = corner[0, 0], corner[1, 0]
         elif e < 11:
-            row, r, dl = base[e - 3].astype(F32), e - 3, 0
+            row, r = base[e - 3].astype(F32), e - 3
+            left, right = lon_recv[3, 2 * DP :], lon_recv[1, 2 * DP :]
         else:
-            row, r, dl = rows_recv[e - 8].astype(F32), e - 11, -1
-        left = pltpu.roll(edge_recv[0, dl + 1].astype(F32), (-3 * r) % 128, 1)
-        right = pltpu.roll(edge_recv[1, dl + 1].astype(F32), (107 - 3 * r) % 128, 1)
+            row, r = rows_recv[e - 8].astype(F32), e - 11
+            left, right = corner[0, 1], corner[1, 1]
+        left = pltpu.roll(left.astype(F32), (-3 * r) % 128, 1)
+        right = pltpu.roll(right.astype(F32), (107 - 3 * r) % 128, 1)
         first = jnp.where(lane < 3, left, row[:, :128])
         last = jnp.where(lane >= 107, right, row[:, 256:])
         last = jnp.where(lane >= 110, 0.0, last)
@@ -293,37 +315,42 @@
             row = row * jnp.where(lat == 0, 0.0, 1.0)
         if e >= 11:
             row = row * jnp.where(lat == N_LAT - 1, 0.0, 1.0)
+        seas[e] = row[STATE : STATE + 1]
+        row = row.astype(BF16)
         if e < 3 or e >= 11:
-            own_columns(row.astype(BF16), e)
-        flux_row = (0, 0, 0, 1, 1, 1, 1, 2, 2, 2, 2, 3, 3, 3)[e]
-        flux = up_flux[8 * flux_row : 8 * flux_row + 8] * row[STATE : STATE + 1]
-        pairs = [(p, h) for p, h in ((e, 0), (e - 1, 1)) if 0 <= p < 13]
-        quads = [(13 + e - h, h) for h in range(4) if 0 <= e - h < 11]
-        inner, outer = [], []
+            own_columns(row, e)
         for v in range(7):
-            shifted = wrapped(row[:, :128], row[:, 256:], v, lane).astype(BF16)
-            for p, h in quads:
-                xs[p, SP * v : SP * (v + 1), 128 * h : 128 * (h + 1)] = shifted
-            inner.append(pltpu.roll(flux, WIDE - 52 - v, 1)[:, :256])
-            outer.append(wrapped(flux[:, :128], flux[:, 256:], v, flux_lane))
-        inner = jnp.concatenate(inner + [put_zeros(8, 256)], axis=0).astype(BF16)
-        outer = jnp.concatenate(outer + [put_zeros(8, 128)], axis=0).astype(BF16)
-        for p, h in pairs:
-            xf[p, :, 256 * h : 256 * (h + 1)] = inner
-        for p, h in quads:
-            xf[p, :, 128 * h : 128 * (h + 1)] = outer
-            xs[p, 7 * SP : 7 * SP + KF, 128 * h : 128 * (h + 1)] = outer
-
-    def rest(u, rows, first):
-        weights = jnp.concatenate([w_all[:, KS * u : KS * u + rows.shape[0]], w_flux[...]], axis=1)
-        return dot(weights, jnp.concatenate([rows, xf[first : first + 7].reshape(7 * KF, 512)], axis=0))
-
-    acc[0, :, :512] += rest(0, stack(0, 3), 0)
-    acc[0, :, 512:] += rest(0, stack(2, 1), 2)
-    acc[1, :, :512] += rest(6, stack(10, 1), 4)
-    acc[1, :, 512:] += rest(4, stack(10, 3), 6)
+            shifted = ring(row, v)
+            for h in range(4):
+                if 0 <= e - h < 11:
+                    xs[13 + e - h, SP * v : SP * (v + 1), 128 * h : 128 * (h + 1)] = shifted
+        if 3 <= e < 11:
+            i = (e - 3) // 4
+            put_flux(e, up_flux[8 * i : 8 * i + 8] * seas[e])
+
+    for e in (0, 1, 2):
+        place(e)
+    acc[0, :, :512] += dot(w_all[:, : 3 * KS], stack(0, 3))
+    acc[0, :, 512:] += dot(w_all[:, :KS], stack(2, 1))
+    for e in (11, 12, 13):
+        place(e)
+    acc[1, :, :512] += dot(w_all[:, 6 * KS :], stack(10, 1))
+    acc[1, :, 512:] += dot(w_all[:, 4 * KS :], stack(10, 3))
+    for e in range(3, 11):
+        place(e)
+    for copy in flux_copies:
+        copy.wait_recv()
+    for e in (0, 1, 2, 11, 12, 13):
+        put_flux(e, flux_recv[0 if e < 3 else 1] * seas[e])
+
+    def flux_stack(first):
+        return xf[first : first + 7].reshape(7 * KF, 512)
+
     acc[2, :, :512] = dot(w_all[...], stack(13, 7))
     acc[2, :, 512:] = dot(w_all[...], stack(17, 7))
+    for g in range(2):
+        sides = jnp.concatenate([flux_stack(4 * g), flux_stack(4 * g + 2)], axis=1)
+        acc[g] += dot(w_flux[...], sides)
 
     def group(g, carry):
         conv = acc[g]
@@ -332,15 +359,16 @@
         variance = jnp.sum(centered * centered, axis=0, keepdims=True) * (1.0 / CH)
         scale = jnp.concatenate([gains[...]] * 8, axis=1)
         normed = (centered * lax.rsqrt(variance + 1e-6) * scale).astype(BF16)
-        hidden[:HID] = gelu(dot(w_wide[...], normed)).astype(BF16)
+        hidden[g, :HID] = gelu(dot(w_wide[...], normed)).astype(BF16)
         for h in range(2):
-            p = jnp.where(g < 2, 4 * g + 2 * h, 13 + 4 * h) + 3
-            hidden[HID : HID + SP, 512 * h : 512 * (h + 1)] = xs[p, 3 * SP : 4 * SP]
-            hidden[HID + SP :, 512 * h : 512 * (h + 1)] = xf[p]
-        fresh[g] = hidden[HID : HID + SP].astype(F32) + dot(w_out[...], hidden[...])
+            p = (4 * g + 2 * h if g < 2 else 13 + 4 * h) + 3
+            hidden[g, HID : HID + SP, 512 * h : 512 * (h + 1)] = xs[p, 3 * SP : 4 * SP]
+            hidden[g, HID + SP :, 512 * h : 512 * (h + 1)] = xf[p]
+        fresh[g] = hidden[g, HID : HID + SP].astype(F32) + dot(w_out[...], hidden[g])
         return carry
 
-    lax.fori_loop(0, 3, group, 0)
+    for g in range(3):
+        group(g, 0)
 
     def fresh_row(r, rows):
         inner = fresh[r // 4, :rows, 256 * (r % 4) : 256 * (r % 4 + 1)]
@@ -404,20 +432,11 @@
     both = part[...] + part_twin[...]
     pair[...] = both
 
-    def slot_of(y, z):
-        return lax.rem(y, 2) * 8 + (y // 2) * 4 + z
-
-    mine = slot_of(chip_y, lon)
-    chips[core * 16 + (1 - core) * mine] = both
-    chip_copies = []
-    for dy, dz in ((2, 2), (2, 1), (2, 3), (0, 2), (2, 0), (0, 1), (0, 3)):
-        chip_copies.append(send(pair, chips.at[mine], (0, 2 * (dy + core), dz)))
-    chip_copies.append(send(pair, chips.at[core * mine + (1 - core) * 17], (0, 2, 0)))
+    mine = chip_y * N_LON + lon
+    chips[mine] = both
+    chip_copies = [send(pair, chips.at[mine], (0, 2 * dy, k)) for dy, k in CHIP_MOVES]
     for copy in chip_copies:
         copy.wait_recv()
-    here = pl.ds(lax.rem(chip_y + core, 2) * 8, 8)
-    half_copy = send(chips.at[here], chips.at[here], twin)
-    half_copy.wait_recv()
     total = chips[0]
     for m in range(1, 16):
         total = total + chips[m]
@@ -429,13 +448,9 @@
     out_copy.wait()
 
 
-FAR_PARTNERS = list(
-    zip(
-        [(4, 0), (4, 1), (4, 2), (4, 3), (2, 0), (6, 0), (2, 1), (6, 3)],
-        [(2, 0), (2, 1), (2, 2), (2, 3), (6, 0), (6, 1), (6, 2), (6, 3)],
-    )
-)
-N_COPIES = len(DRIVER_MOVES) + len(ROW_MOVES) + len(EDGE_MOVES) + 3 + 1 + 8 + 1
+CHIP_MOVES = [(2, 2), (2, 1), (2, 3), (1, 2), (3, 2), (2, 0), (0, 2), (1, 1), (1, 3), (3, 1), (3, 3)]
+CHIP_MOVES += [(1, 0), (3, 0), (0, 1), (0, 3)]
+N_COPIES = len(LON_MOVES) + len(ROW_MOVES) + len(CORNER_MOVES) + 2 + 3 + 1 + 15
 
 
 def hand_over(*refs):
@@ -469,11 +484,12 @@
         + [
             pltpu.VMEM((SP, ROWS, WIDE), F32),
             pltpu.VMEM((ROWS, SP, WIDE), BF16),
-            pltpu.VMEM((2, SP, 128), BF16),
-            pltpu.VMEM((2, 3, SP, 128), BF16),
+            pltpu.VMEM((2, 2 * DP + SP, 128), BF16),
+            pltpu.VMEM((N_LON, 2 * DP + SP, 128), BF16),
+            pltpu.VMEM((2, 2, SP, 128), BF16),
             pltpu.VMEM((6, SP, WIDE), BF16),
-            pltpu.VMEM((2, DP, 128), BF16),
-            pltpu.VMEM((N_LON, 4, DP, 128), BF16),
+            pltpu.VMEM((2, 8, WIDE), F32),
+            pltpu.VMEM((2, 8, WIDE), F32),
             pltpu.VMEM((CP, 7 * KS), BF16),
             pltpu.VMEM((CP, 7 * KF), BF16),
             pltpu.VMEM((HID, CP), BF16),
@@ -485,7 +501,7 @@
             pltpu.VMEM((24, KS, 512), BF16),
             pltpu.VMEM((24, KF, 512), BF16),
             pltpu.VMEM((3, CP, 1024), F32),
-            pltpu.VMEM((HK, 1024), BF16),
+            pltpu.VMEM((3, HK, 1024), BF16),
             pltpu.VMEM((3, SP, 1024), F32),
             pltpu.VMEM((STATE, ROWS, COLS), BF16),
             pltpu.VMEM((ROWS, WIDE), F32),
@@ -493,7 +509,7 @@
             pltpu.VMEM((8, 128), F32),
             pltpu.VMEM((8, 128), F32),
             pltpu.VMEM((8, 128), F32),
-            pltpu.VMEM((18, 8, 128), F32),
+            pltpu.VMEM((16, 8, 128), F32),
             pltpu.SemaphoreType.DMA((len(operands),)),
             pltpu.SemaphoreType.DMA,
             pltpu.SemaphoreType.DMA((N_COPIES,)),

time: 43.2 us -> 41.5 us (0.961)
  Pallas kernels: 42.4 us -> 40.7 us
    pallas_call x1, Pallas kernels: 40 us -> 38.3 us  [on_device(): pl.pallas_call(kernel, out_shape=outputs, in_specs=[anywhere] * len(opera...]
where the time goes in v3:
time: 41.5 us; the launch traced here: 41.3 us
  Pallas kernels  40.7 us (98%)
  between operations  0.65 us (2%)
    pallas_call x1, Pallas kernels, on_device(): pl.pallas_call(kernel, out_shape=outputs, in_specs=[anywhere] * len(opera...  38.3 us
    pallas_call x1, Pallas kernels, on_device(): pl.pallas_call(hand_over, out_shape=outputs, in_specs=[vmem] * 4, out_spe...  2.42 us

profile of v3, /device:TPU:1, one launch (start us, length us, event | category | flops | bytes accessed | tf_op | source)
XLA Modules:
  0.0 41.3 jit_solution(10131069936666417501)
XLA Ops:
  0.6 38.3 %coupled_step.1 = (bf16[77,8,360]{2,1,0:T(8,128)(2,1)}, f32[2,90]{1,0:T(2,128)}, f32[8,360]{1,0:T(8,128)}, f32[1,1]{1,0:T(1,128)}) custom-call(bf16[77,8,360]{2,1,0:T(8,128)(2,1)} %bitcast.9, s32[8,360]{1,0:T(8,128)} %flags_h.1, s32[1,30]{1,0:T(1,128)} %tiles_h.1, f32[8,360]{1,0:T(8,128)} %heat_h.1, bf16[40,2,90]{2,1,0:T(2,128)(2,1)} %bitcast.11, ...), custom_call_target="tpu_custom_call" | custom-call | tf_op jit(solution)/shard_map/coupled_step/pallas_call | solution.py:478
  38.9 2.4 %hand_over.1 = (bf16[77,8,360]{2,1,0:T(8,128)(2,1)}, f32[2,90]{1,0:T(2,128)}, f32[8,360]{1,0:T(8,128)}, f32[1,1]{1,0:T(1,128)}) custom-call(bf16[77,8,360]{2,1,0:T(8,128)(2,1)} %get-tuple-element.12.refs_0_, f32[2,90]{1,0:T(2,128)} %get-tuple-element.13.refs_1_, f32[8,360]{1,0:T(8,128)} %get-tuple-element.14.refs_2_, f32[1,1]{1,0:T(1,128)} %get-tuple-element.15.refs_3_), custom_call_target="tpu_custom_call" | custom-call | tf_op jit(solution)/shard_map/hand_over/pallas_call | solution.py:523

commit v4 on v3

--- a/solution.py
+++ b/solution.py
@@ -91,7 +91,7 @@
     air, inphase, quadrature, exchange, intake, stencil, gain, widening, narrowing, readout,
     grid, base, pack, lon_recv, corner, rows_recv, flux_send, flux_recv,
     w_all, w_flux, w_wide, w_out, gains, w_atm, w_lift, w_exch,
-    xs, xf, acc, hidden, fresh, out_buf, x_own, x_all, part, part_twin, pair, chips,
+    xs, xf, acc, hidden, fresh, out_buf, x_own, x_all, terms, pair, chips,
     load_sem, out_sem, send_sem, recv_sem,
 ):
     sec, lat, lon = lax.axis_index("sec"), lax.axis_index("lat"), lax.axis_index("lon")
@@ -107,6 +107,8 @@
 
     partners = []
     partners += [(0, 2 * dy, k) for dy in (2, 1, 3) for k in range(N_LON)]
+    twin = 1 - 2 * core
+    partners += [(ds, twin, 0) for ds in range(1, N_SEC)]
     partners += [(0, dl, k) for dl, k in LON_MOVES + CORNER_MOVES + ROW_MOVES] + [(ds, 0, 0) for ds in range(1, N_SEC)]
     barrier = pltpu.get_barrier_semaphore()
     for step in partners:
@@ -225,6 +227,17 @@
     acc[1, :, :512] = dot(w_all[:, : 6 * KS], stack(4, 6))
     acc[1, :, 512:] = dot(w_all[:, : 4 * KS], stack(6, 4))
 
+    loaded(tiles, area, heat)
+    tile = iota((32, WIDE), 0) * 12
+    column = iota((32, WIDE), 1)
+    widen_tiles = jnp.where((column >= tile) & (column < tile + 12), 1.0, 0.0).astype(BF16)
+    marks = padded_to(tiles[...].astype(F32), 1, 32)
+    marked = dot(jnp.broadcast_to(marks, (8, 32)).astype(BF16), widen_tiles)
+    mask = padded_to(sea, ROWS, WIDE) * marked
+    terms[0, 0] = jnp.concatenate([area[lat]] * 3, axis=1) * mask
+    terms[0, 1] = padded_to(heat[...], ROWS, WIDE)
+    terms_copy = send(terms.at[0], terms.at[1], (0, twin, 0))
+
     loaded(widening, narrowing, readout, gain)
     w_wide[...] = turned(widening[...].astype(F32), WIDE, 1280)[:HID, :CP].astype(BF16)
     read = padded_to(readout[...].astype(F32), SP, CH).astype(BF16)
@@ -292,7 +305,6 @@
         for h in range(4):
             if 0 <= e - h < 11:
                 xf[13 + e - h, :, 128 * h : 128 * (h + 1)] = outer
-                xs[13 + e - h, 7 * SP : 7 * SP + KF, 128 * h : 128 * (h + 1)] = outer
 
     seas = {}
     def place(e):
@@ -338,6 +350,8 @@
     acc[1, :, 512:] += dot(w_all[:, 4 * KS :], stack(10, 3))
     for e in range(3, 11):
         place(e)
+    acc[2, :, :512] = dot(w_all[...], stack(13, 7))
+    acc[2, :, 512:] = dot(w_all[...], stack(17, 7))
     for copy in flux_copies:
         copy.wait_recv()
     for e in (0, 1, 2, 11, 12, 13):
@@ -346,10 +360,9 @@
     def flux_stack(first):
         return xf[first : first + 7].reshape(7 * KF, 512)
 
-    acc[2, :, :512] = dot(w_all[...], stack(13, 7))
-    acc[2, :, 512:] = dot(w_all[...], stack(17, 7))
-    for g in range(2):
-        sides = jnp.concatenate([flux_stack(4 * g), flux_stack(4 * g + 2)], axis=1)
+    for g, first in ((0, 0), (1, 4), (2, 13)):
+        second = first + (2 if g < 2 else 4)
+        sides = jnp.concatenate([flux_stack(first), flux_stack(second)], axis=1)
         acc[g] += dot(w_flux[...], sides)
 
     def group(g, carry):
@@ -375,19 +388,13 @@
         outer = fresh[2, :rows, 128 * r : 128 * (r + 1)]
         return jnp.concatenate([inner, outer], axis=1)
 
-    loaded(tiles)
-    tile = iota((32, WIDE), 0) * 12
-    column = iota((32, WIDE), 1)
-    widen_tiles = jnp.where((column >= tile) & (column < tile + 12), 1.0, 0.0).astype(BF16)
-    marks = padded_to(tiles[...].astype(F32), 1, 32)
-    marked = dot(jnp.broadcast_to(marks, (8, 32)).astype(BF16), widen_tiles)
-    mask = padded_to(sea, ROWS, WIDE) * marked
     x_new = jnp.concatenate([fresh_row(r, 8)[:1] for r in range(ROWS)], axis=0)
     x_new = pltpu.roll(x_new, 52, 1).astype(BF16).astype(F32)
     x = jnp.where(mask > 0.5, x_new, padded_to(state[0].astype(F32), ROWS, WIDE))
     x_own[...] = x
-    x_all[sec] = x
-    x_copies = [send(x_own, x_all.at[sec], (ds, 0, 0)) for ds in (2, 1, 3)]
+    x_all[0, sec] = x
+    x_copies = [send(x_own, x_all.at[0, sec], (ds, 0, 0)) for ds in (2, 1, 3)]
+    x_copies += [send(x_own, x_all.at[1, sec], (ds, twin, 0)) for ds in (2, 1, 3, 0)]
 
     for r in range(ROWS):
         grid[:, r, :] = pltpu.roll(fresh_row(r, SP), 52, 1)
@@ -405,33 +412,29 @@
         total = jnp.sum(heat_boxes[4 * i : 4 * i + 4], axis=0, keepdims=True)
         count = jnp.sum(count_boxes[4 * i : 4 * i + 4], axis=0, keepdims=True)
         pooled[i : i + 1, :] = (total / jnp.maximum(count, 1.0))[:, :90]
-    loaded(area, heat)
-    weight = jnp.concatenate([area[lat]] * 3, axis=1) * mask
-    seen = padded_to(heat[...], ROWS, WIDE)
-
     def folded(y):
         return jnp.sum(y[:, :128] + y[:, 128:256] + y[:, 256:], axis=0, keepdims=True)
 
-    area_sum = folded(weight)
+    terms_copy.wait_recv()
+    area_sum = folded(terms[0, 0]) + folded(terms[1, 0])
+
+    def fair_score(which):
+        members = [x_all[which, m] for m in range(N_SEC)]
+        deviation = sum(jnp.abs(m - terms[which, 1]) for m in members)
+        gaps = sum(
+            jnp.abs(members[m] - members[n]) for m in range(N_SEC) for n in range(m + 1, N_SEC)
+        )
+        epsilon = 0.05 / N_SEC
+        return deviation * (1.0 / N_SEC) - (1.0 - epsilon) / (N_SEC * (N_SEC - 1)) * gaps
 
     for copy in x_copies:
         copy.wait_recv()
-    members = [x_all[m] for m in range(N_SEC)]
-    deviation = sum(jnp.abs(m - seen) for m in members)
-    gaps = sum(
-        jnp.abs(members[m] - members[n]) for m in range(N_SEC) for n in range(m + 1, N_SEC)
-    )
-    epsilon = 0.05 / N_SEC
-    fair = deviation * (1.0 / N_SEC) - (1.0 - epsilon) / (N_SEC * (N_SEC - 1)) * gaps
+    fair = fair_score(0)
     score[...] = fair[:, :COLS]
 
-    part[...] = jnp.concatenate([folded(weight * fair), area_sum, put_zeros(6, 128)], axis=0)
-    twin = (0, 1 - 2 * core, 0)
-    twin_copy = send(part, part_twin, twin)
-    twin_copy.wait_recv()
-    both = part[...] + part_twin[...]
+    heat_sum = folded(terms[0, 0] * fair) + folded(terms[1, 0] * fair_score(1))
+    both = jnp.concatenate([heat_sum, area_sum, put_zeros(6, 128)], axis=0)
     pair[...] = both
-
     mine = chip_y * N_LON + lon
     chips[mine] = both
     chip_copies = [send(pair, chips.at[mine], (0, 2 * dy, k)) for dy, k in CHIP_MOVES]
@@ -450,7 +453,7 @@
 
 CHIP_MOVES = [(2, 2), (2, 1), (2, 3), (1, 2), (3, 2), (2, 0), (0, 2), (1, 1), (1, 3), (3, 1), (3, 3)]
 CHIP_MOVES += [(1, 0), (3, 0), (0, 1), (0, 3)]
-N_COPIES = len(LON_MOVES) + len(ROW_MOVES) + len(CORNER_MOVES) + 2 + 3 + 1 + 15
+N_COPIES = len(LON_MOVES) + len(ROW_MOVES) + len(CORNER_MOVES) + 2 + 1 + 7 + 15
 
 
 def hand_over(*refs):
@@ -505,9 +508,8 @@
             pltpu.VMEM((3, SP, 1024), F32),
             pltpu.VMEM((STATE, ROWS, COLS), BF16),
             pltpu.VMEM((ROWS, WIDE), F32),
-            pltpu.VMEM((N_SEC, ROWS, WIDE), F32),
-            pltpu.VMEM((8, 128), F32),
-            pltpu.VMEM((8, 128), F32),
+            pltpu.VMEM((2, N_SEC, ROWS, WIDE), F32),
+            pltpu.VMEM((2, 2, ROWS, WIDE), F32),
             pltpu.VMEM((8, 128), F32),
             pltpu.VMEM((16, 8, 128), F32),
             pltpu.SemaphoreType.DMA((len(operands),)),

time: 41.5 us -> 40.4 us (0.973)
  Pallas kernels: 40.7 us -> 39.6 us
    pallas_call x1, Pallas kernels: 38.3 us -> 37.2 us  [on_device(): pl.pallas_call(kernel, out_shape=outputs, in_specs=[anywhere] * len(opera...]
where the time goes in v4:
time: 40.4 us; the launch traced here: 40.2 us
  Pallas kernels  39.6 us (98%)
  between operations  0.65 us (2%)
    pallas_call x1, Pallas kernels, on_device(): pl.pallas_call(kernel, out_shape=outputs, in_specs=[anywhere] * len(opera...  37.2 us
    pallas_call x1, Pallas kernels, on_device(): pl.pallas_call(hand_over, out_shape=outputs, in_specs=[vmem] * 4, out_spe...  2.42 us

profile of v4, /device:TPU:1, one launch (start us, length us, event | category | flops | bytes accessed | tf_op | source)
XLA Modules:
  0.0 40.2 jit_solution(8067527851427241237)
XLA Ops:
  0.6 37.2 %coupled_step.1 = (bf16[77,8,360]{2,1,0:T(8,128)(2,1)}, f32[2,90]{1,0:T(2,128)}, f32[8,360]{1,0:T(8,128)}, f32[1,1]{1,0:T(1,128)}) custom-call(bf16[77,8,360]{2,1,0:T(8,128)(2,1)} %bitcast.9, s32[8,360]{1,0:T(8,128)} %flags_h.1, s32[1,30]{1,0:T(1,128)} %tiles_h.1, f32[8,360]{1,0:T(8,128)} %heat_h.1, bf16[40,2,90]{2,1,0:T(2,128)(2,1)} %bitcast.11, ...), custom_call_target="tpu_custom_call" | custom-call | tf_op jit(solution)/shard_map/coupled_step/pallas_call | solution.py:481
  37.8 2.4 %hand_over.1 = (bf16[77,8,360]{2,1,0:T(8,128)(2,1)}, f32[2,90]{1,0:T(2,128)}, f32[8,360]{1,0:T(8,128)}, f32[1,1]{1,0:T(1,128)}) custom-call(bf16[77,8,360]{2,1,0:T(8,128)(2,1)} %get-tuple-element.12.refs_0_, f32[2,90]{1,0:T(2,128)} %get-tuple-element.13.refs_1_, f32[8,360]{1,0:T(8,128)} %get-tuple-element.14.refs_2_, f32[1,1]{1,0:T(1,128)} %get-tuple-element.15.refs_3_), custom_call_target="tpu_custom_call" | custom-call | tf_op jit(solution)/shard_map/hand_over/pallas_call | solution.py:525

commit v5 on v4

--- a/solution.py
+++ b/solution.py
@@ -201,7 +201,7 @@
     chan = iota((128, KS), 0)
     intake_rep = dot(intake_t, jnp.where(chan == source, 1.0, 0.0).astype(BF16))
     chan = iota((64, KS), 0) - tap
-    for u in range(7):
+    def build(u):
         taps = dot(stencil_t, jnp.where(chan == 7 * u, 1.0, 0.0).astype(BF16))
         product = taps * intake_rep
         w_all[:, KS * u : KS * (u + 1)] = product.astype(BF16)
@@ -216,16 +216,23 @@
             for p, h in places:
                 xs[p, SP * v : SP * (v + 1), 256 * h : 256 * (h + 1)] = shifted
 
-    for e in range(3, 11):
-        own_columns(base[e - 3], e)
-
     def stack(first, count):
         return xs[first : first + count].reshape(count * KS, 512)
 
+    for u in range(4):
+        build(u)
+    for e in range(6, 11):
+        own_columns(base[e - 3], e)
+    acc[1, :, 512:] = dot(w_all[:, : 4 * KS], stack(6, 4))
+    for u in (4, 5):
+        build(u)
+    for e in (4, 5):
+        own_columns(base[e - 3], e)
+    acc[1, :, :512] = dot(w_all[:, : 6 * KS], stack(4, 6))
+    build(6)
+    own_columns(base[0], 3)
     acc[0, :, :512] = dot(w_all[:, 3 * KS :], stack(3, 4))
     acc[0, :, 512:] = dot(w_all[:, KS:], stack(3, 6))
-    acc[1, :, :512] = dot(w_all[:, : 6 * KS], stack(4, 6))
-    acc[1, :, 512:] = dot(w_all[:, : 4 * KS], stack(6, 4))
 
     loaded(tiles, area, heat)
     tile = iota((32, WIDE), 0) * 12
@@ -372,7 +379,8 @@
         variance = jnp.sum(centered * centered, axis=0, keepdims=True) * (1.0 / CH)
         scale = jnp.concatenate([gains[...]] * 8, axis=1)
         normed = (centered * lax.rsqrt(variance + 1e-6) * scale).astype(BF16)
-        hidden[g, :HID] = gelu(dot(w_wide[...], normed)).astype(BF16)
+        wide = dot(w_wide[...], normed).astype(BF16)
+        hidden[g, :HID] = (wide * jnp.bfloat16(0.5)) * (1 + lax.erf(wide * jnp.bfloat16(0.5**0.5)))
         for h in range(2):
             p = (4 * g + 2 * h if g < 2 else 13 + 4 * h) + 3
             hidden[g, HID : HID + SP, 512 * h : 512 * (h + 1)] = xs[p, 3 * SP : 4 * SP]
@@ -380,7 +388,7 @@
         fresh[g] = hidden[g, HID : HID + SP].astype(F32) + dot(w_out[...], hidden[g])
         return carry
 
-    for g in range(3):
+    for g in (2, 0, 1):
         group(g, 0)
 
     def fresh_row(r, rows):
@@ -430,7 +438,6 @@
     for copy in x_copies:
         copy.wait_recv()
     fair = fair_score(0)
-    score[...] = fair[:, :COLS]
 
     heat_sum = folded(terms[0, 0] * fair) + folded(terms[1, 0] * fair_score(1))
     both = jnp.concatenate([heat_sum, area_sum, put_zeros(6, 128)], axis=0)
@@ -438,6 +445,7 @@
     mine = chip_y * N_LON + lon
     chips[mine] = both
     chip_copies = [send(pair, chips.at[mine], (0, 2 * dy, k)) for dy, k in CHIP_MOVES]
+    score[...] = fair[:, :COLS]
     for copy in chip_copies:
         copy.wait_recv()
     total = chips[0]

time: 40.4 us -> 39.9 us (0.988)
    pallas_call x1, Pallas kernels: 37.2 us -> 36.7 us  [on_device(): pl.pallas_call(kernel, out_shape=outputs, in_specs=[anywhere] * len(opera...]
where the time goes in v5:
time: 39.9 us; the launch traced here: 39.8 us
  Pallas kernels  39.2 us (98%)
  between operations  0.65 us (2%)
    pallas_call x1, Pallas kernels, on_device(): pl.pallas_call(kernel, out_shape=outputs, in_specs=[anywhere] * len(opera...  36.7 us
    pallas_call x1, Pallas kernels, on_device(): pl.pallas_call(hand_over, out_shape=outputs, in_specs=[vmem] * 4, out_spe...  2.42 us

profile of v5, /device:TPU:1, one launch (start us, length us, event | category | flops | bytes accessed | tf_op | source)
XLA Modules:
  0.0 39.8 jit_solution(14664353030217987691)
XLA Ops:
  0.6 36.7 %coupled_step.1 = (bf16[77,8,360]{2,1,0:T(8,128)(2,1)}, f32[2,90]{1,0:T(2,128)}, f32[8,360]{1,0:T(8,128)}, f32[1,1]{1,0:T(1,128)}) custom-call(bf16[77,8,360]{2,1,0:T(8,128)(2,1)} %bitcast.9, s32[8,360]{1,0:T(8,128)} %flags_h.1, s32[1,30]{1,0:T(1,128)} %tiles_h.1, f32[8,360]{1,0:T(8,128)} %heat_h.1, bf16[40,2,90]{2,1,0:T(2,128)(2,1)} %bitcast.11, ...), custom_call_target="tpu_custom_call" | custom-call | tf_op jit(solution)/shard_map/coupled_step/pallas_call | solution.py:489
  37.4 2.4 %hand_over.1 = (bf16[77,8,360]{2,1,0:T(8,128)(2,1)}, f32[2,90]{1,0:T(2,128)}, f32[8,360]{1,0:T(8,128)}, f32[1,1]{1,0:T(1,128)}) custom-call(bf16[77,8,360]{2,1,0:T(8,128)(2,1)} %get-tuple-element.12.refs_0_, f32[2,90]{1,0:T(2,128)} %get-tuple-element.13.refs_1_, f32[8,360]{1,0:T(8,128)} %get-tuple-element.14.refs_2_, f32[1,1]{1,0:T(1,128)} %get-tuple-element.15.refs_3_), custom_call_target="tpu_custom_call" | custom-call | tf_op jit(solution)/shard_map/hand_over/pallas_call | solution.py:533

commit v6 on v5

--- a/solution.py
+++ b/solution.py
@@ -375,8 +375,11 @@
     def group(g, carry):
         conv = acc[g]
         mean = jnp.sum(conv, axis=0, keepdims=True) * (1.0 / CH)
-        centered = jnp.where(iota((CP, 1024), 0) < CH, conv - mean, 0.0)
-        variance = jnp.sum(centered * centered, axis=0, keepdims=True) * (1.0 / CH)
+        centered = conv - mean
+        square = centered * centered
+        end = jnp.where(iota((8, 1024), 0) < CH - (CP - 8), square[CP - 8 :], 0.0)
+        variance = jnp.sum(square[: CP - 8], axis=0, keepdims=True)
+        variance = (variance + jnp.sum(end, axis=0, keepdims=True)) * (1.0 / CH)
         scale = jnp.concatenate([gains[...]] * 8, axis=1)
         normed = (centered * lax.rsqrt(variance + 1e-6) * scale).astype(BF16)
         wide = dot(w_wide[...], normed).astype(BF16)

time: 39.9 us -> 39.9 us (level)
  no operation moved by 1% of the time
where the time goes in v6:
time: 39.9 us; the launch traced here: 39.8 us
  Pallas kernels  39.1 us (98%)
  between operations  0.65 us (2%)
    pallas_call x1, Pallas kernels, on_device(): pl.pallas_call(kernel, out_shape=outputs, in_specs=[anywhere] * len(opera...  36.7 us
    pallas_call x1, Pallas kernels, on_device(): pl.pallas_call(hand_over, out_shape=outputs, in_specs=[vmem] * 4, out_spe...  2.42 us

profile of v6, /device:TPU:1, one launch (start us, length us, event | category | flops | bytes accessed | tf_op | source)
XLA Modules:
  0.0 39.8 jit_solution(12395886584562030851)
XLA Ops:
  0.6 36.7 %coupled_step.1 = (bf16[77,8,360]{2,1,0:T(8,128)(2,1)}, f32[2,90]{1,0:T(2,128)}, f32[8,360]{1,0:T(8,128)}, f32[1,1]{1,0:T(1,128)}) custom-call(bf16[77,8,360]{2,1,0:T(8,128)(2,1)} %bitcast.9, s32[8,360]{1,0:T(8,128)} %flags_h.1, s32[1,30]{1,0:T(1,128)} %tiles_h.1, f32[8,360]{1,0:T(8,128)} %heat_h.1, bf16[40,2,90]{2,1,0:T(2,128)(2,1)} %bitcast.11, ...), custom_call_target="tpu_custom_call" | custom-call | tf_op jit(solution)/shard_map/coupled_step/pallas_call | solution.py:492
  37.3 2.4 %hand_over.1 = (bf16[77,8,360]{2,1,0:T(8,128)(2,1)}, f32[2,90]{1,0:T(2,128)}, f32[8,360]{1,0:T(8,128)}, f32[1,1]{1,0:T(1,128)}) custom-call(bf16[77,8,360]{2,1,0:T(8,128)(2,1)} %get-tuple-element.12.refs_0_, f32[2,90]{1,0:T(2,128)} %get-tuple-element.13.refs_1_, f32[8,360]{1,0:T(8,128)} %get-tuple-element.14.refs_2_, f32[1,1]{1,0:T(1,128)} %get-tuple-element.15.refs_3_), custom_call_target="tpu_custom_call" | custom-call | tf_op jit(solution)/shard_map/hand_over/pallas_call | solution.py:536
